TPU v7x, 128 devices: a whole 4x4x4 slice. The times are simulated.
128 devices in a mesh: dp: 8 (over x_hi, y), vocab: 16 (over x_lo, z, core).
Axes of the slice: x: 4 (x_hi: 2, x_lo: 2; x = x_hi * 2 + x_lo), y: 4, z: 4, core: 2. Of those that a mesh axis runs over, the one named last changes fastest.
Arguments:
- hidden: bfloat16 [8192, 4096], P('dp', 'vocab'), may hold values from -6 to 6
- norm_gain: float32 [4096], replicated, may hold values from 0.5 to 3
- head_weight: bfloat16 [4096, 16000], P(None, 'vocab')
- lengths: int32 [64], P('dp'), may hold values from 16 to 128
- positives: int32 [16], P('dp'), may hold values from 0 to 47
- negatives: int32 [16, 2], P('dp'), may hold values from 0 to 47
Outputs:
- losses: float32 [3], replicated
- hidden_grad: bfloat16 [8192, 4096], P('dp', 'vocab')
- head_grad: bfloat16 [4096, 16000], P('dp', 'vocab')
- gain_grad: float32 [4096], P('vocab')
All inputs are finite; a program needn't handle non-finite values.
Results may differ from a plain program's by a relative error of at most 0.025.
Values may be sent and summed in bfloat16 or wider, within the bound.
No kernel may reach another device: no remote copies, remote signals or barrier semaphores. Data moves between devices by JAX's collectives and lax.ppermute only.
A program may use at most 128 MiB of HBM per device.

v0:
```python
import math

import jax
import jax.numpy as jnp
from jax import lax
from jax.sharding import PartitionSpec as P

VOCAB = 16000


epsilon = 1e-05
sharpness = 80.0
flops_weight = 0.01


def contrast(scores, positive_ids, negative_ids):
    query_count = scores.shape[0]
    passage_count = scores.shape[1]
    negative_count = negative_ids.shape[1]
    columns = jnp.arange(passage_count, dtype=jnp.int32)
    positive_hot = (columns[None, :] == positive_ids[:, None]).astype(jnp.float32)
    negative_hot = (columns[None, None, :] == negative_ids[:, :, None]).astype(jnp.float32)
    highest = jnp.max(scores, axis=1, keepdims=True)
    shifted = jnp.exp(scores - highest)
    denominator = jnp.sum(shifted, axis=1, keepdims=True)
    log_total = highest[:, 0] + jnp.log(denominator[:, 0])
    positive_score = jnp.sum(scores * positive_hot, axis=1)
    negative_score = jnp.sum(scores[:, None, :] * negative_hot, axis=2)
    margins = negative_score - positive_score[:, None]
    cross_loss = jnp.mean(log_total - positive_score)
    margin_loss = jnp.mean(jax.nn.softplus(margins))
    slopes = jax.nn.sigmoid(margins) / (query_count * negative_count)
    score_grad = (shifted / denominator - positive_hot) / query_count
    score_grad = score_grad + jnp.sum(slopes[:, :, None] * negative_hot, axis=1)
    score_grad = score_grad - jnp.sum(slopes, axis=1)[:, None] * positive_hot
    return (cross_loss, margin_loss, score_grad)


def pool_block(logits, valid):
    seq_count = valid.shape[0]
    activity = jnp.log1p(jnp.maximum(logits, 0.0))
    per_sequence = activity.reshape(seq_count, -1, logits.shape[1])
    valid_cells = valid[:, :, None]
    peak_value = jnp.max(jnp.where(valid_cells, per_sequence, 0.0), axis=1, keepdims=True)
    raised = jnp.where(valid_cells, jnp.exp(sharpness * (per_sequence - peak_value)), 0.0)
    summed = jnp.sum(raised, axis=1, keepdims=True)
    pooled = peak_value[:, 0, :] + jnp.log(summed[:, 0, :]) / sharpness
    return (pooled, raised / summed)


def logit_gradient(logits, weights, rep_grad):
    derivative = jnp.where(logits > 0.0, 1.0 / (1.0 + jnp.maximum(logits, 0.0)), 0.0)
    spread_grad = (rep_grad[:, None, :] * weights).reshape(logits.shape)
    return (spread_grad * derivative).astype(jnp.bfloat16)


def shards(hidden, norm_gain, head_weight, lengths, positives, negatives):
    dp_count = lax.axis_size("dp")
    vocab_index = lax.axis_index("vocab")
    dp_index = lax.axis_index("dp")
    tok_rows, width_local = hidden.shape
    full_width = norm_gain.shape[0]
    vocab_local = head_weight.shape[1]
    seq_count = lengths.shape[0]
    seq_length = tok_rows // seq_count
    query_local = positives.shape[0]
    passage_local = seq_count - query_local
    local_values = hidden.astype(jnp.float32)
    gain_local = lax.dynamic_slice_in_dim(norm_gain, vocab_index * width_local, width_local, 0)
    whole_rows = lax.all_gather(hidden, "vocab", axis=1, tiled=True).astype(jnp.float32)
    inverse = lax.rsqrt(jnp.mean(whole_rows * whole_rows, axis=1, keepdims=True) + epsilon)
    normed = (whole_rows * inverse * norm_gain).astype(jnp.bfloat16)
    logits = jnp.dot(normed, head_weight, preferred_element_type=jnp.float32)
    unit_local = local_values * inverse
    valid = jnp.arange(seq_length, dtype=jnp.int32)[None, :] < lengths[:, None]
    pooled, weights = pool_block(logits, valid)
    pooled_all, positive_all, negative_all = (
        lax.all_gather(pooled, "dp", axis=0, tiled=True),
        lax.all_gather(positives, "dp", axis=0, tiled=True),
        lax.all_gather(negatives, "dp", axis=0, tiled=True),
    )
    grouped = pooled_all.reshape(dp_count, seq_count, vocab_local)
    queries = grouped[:, :query_local].reshape(dp_count * query_local, vocab_local)
    passages = grouped[:, query_local:].reshape(dp_count * passage_local, vocab_local)
    score_scale = 4.0 / math.sqrt(VOCAB)
    part_scores = score_scale * lax.dot_general(
        queries, passages, (((1,), (1,)), ((), ())), precision=lax.Precision.HIGHEST
    )
    mean_rep = jnp.mean(pooled_all, axis=0)
    part_flops = jnp.sum(mean_rep * mean_rep)
    scores, flops_total = lax.psum((part_scores, part_flops), "vocab")
    cross_loss, margin_loss, score_grad = contrast(scores, positive_all, negative_all)
    losses = jnp.stack([cross_loss, margin_loss, flops_weight * flops_total])
    own_queries = lax.dynamic_slice_in_dim(score_grad, dp_index * query_local, query_local, 0)
    own_passages = lax.dynamic_slice_in_dim(score_grad, dp_index * passage_local, passage_local, 1)
    query_grad = score_scale * jnp.dot(own_queries, passages, precision=lax.Precision.HIGHEST)
    passage_grad = score_scale * lax.dot_general(
        own_passages, queries, (((0,), (0,)), ((), ())), precision=lax.Precision.HIGHEST
    )
    rep_grad = jnp.concatenate([query_grad, passage_grad], axis=0)
    rep_grad = rep_grad + 2.0 * flops_weight / (dp_count * seq_count) * mean_rep[None, :]
    local_grad = logit_gradient(logits, weights, rep_grad)
    head_sum = lax.psum_scatter(
        lax.dot_general(
            normed, local_grad, (((0,), (0,)), ((), ())), preferred_element_type=jnp.float32
        ).astype(jnp.bfloat16),
        "dp",
        scatter_dimension=0,
        tiled=True,
    )
    partial_grad = lax.dot_general(
        local_grad, head_weight, (((1,), (1,)), ((), ())), preferred_element_type=jnp.float32
    )
    normed_grad = lax.psum_scatter(
        partial_grad.astype(jnp.bfloat16), "vocab", scatter_dimension=1, tiled=True
    ).astype(jnp.float32)
    scaled_grad = normed_grad * gain_local
    row_total = lax.psum(jnp.sum(scaled_grad * unit_local, axis=1), "vocab")
    gain_grad = lax.psum(jnp.sum(normed_grad * unit_local, axis=0), "dp")
    hidden_grad = (inverse * (scaled_grad - unit_local * (row_total[:, None] / full_width))).astype(
        jnp.bfloat16
    )
    return (losses, hidden_grad, head_sum, gain_grad)


def solution(mesh):
    in_specs = (P("dp", "vocab"), P(), P(None, "vocab"), P("dp"), P("dp"), P("dp", None))
    out_specs = (P(), P("dp", "vocab"), P("dp", "vocab"), P("vocab"))
    return jax.shard_map(shards, mesh=mesh, in_specs=in_specs, out_specs=out_specs, check_vma=False)
```

profile of v0, /device:TPU:0, one launch (start us, length us, event | category | flops | bytes accessed | tf_op | source)
XLA Modules:
  0.0 389.8 jit_solution(14375326638080620326)
XLA Ops:
  7.2 0.0 all-gather.3.cloned.1.call-start
  7.2 0.7 all-gather.3.cloned.1.call-update
  7.9 0.0 reduce-scatter.3.cloned.1.call-start
  8.0 23.9 %all-gather = s32[8,2,2]{2,1,0:T(2,128)S(1)} all-gather(s32[1,2,2]{2,1,0:T(2,128)} %bitcast.59), channel_id=1, replica_groups=mesh['dp'=8,'vocab'=16] {'dp'}, dimensions={0}, use_global_device_ids=true | all-gather | bytes 144 | tf_op jit(solution)/shard_map/all_gather | solution.py:80
  31.9 0.1 copy.33
  31.9 1.2 dynamic-slice
  33.8 0.9 dynamic-update-slice
  34.7 7.9 %all-reduce = s32[16]{0:T(128)S(1)} all-reduce(s32[16]{0:T(128)S(1)} %dynamic-update-slice), channel_id=1, replica_groups=mesh['dp'=8,'vocab'=16] {'dp'}, use_global_device_ids=true, to_apply=%add | all-reduce | flops 16 | bytes 128
  42.6 0.7 fusion.24
  43.3 30.0 %all-gather.3.cloned.1.call-done = bf16[1024,4096]{1,0:T(8,128)(2,1)} async-done(((bf16[1024,256]{1,0:T(8,128)(2,1)}), bf16[1024,4096]{1,0:T(8,128)(2,1)}) %all-gather.3.cloned.1.call-update) | async-done | bytes 8388624 | tf_op jit(solution)/shard_map/all_gather | solution.py:70
  73.3 5.2 %fusion = f32[1024]{0:T(1024)S(1)} fusion(bf16[1024,4096]{1,0:T(8,128)(2,1)} %all-gather.3.cloned.1.call-done), kind=kLoop, calls=%fused_computation.2 | loop fusion | flops 12581888 | bytes 8392704 | tf_op jit(solution)/shard_map/reduce_sum | solution.py:71
  78.5 0.5 copy-done.2
  79.0 12.0 %fusion.10 = f32[1024,1000]{0,1:T(8,128)S(1)} fusion(bf16[4096,1000]{0,1:T(8,128)(2,1)} %param.8, bf16[1024,4096]{1,0:T(8,128)(2,1)S(1)} %copy-done.2, f32[4096]{0:T(1024)S(1)} %copy-done.4, f32[1024]{0:T(1024)S(1)} %add_rsqrt_fusion), kind=kOutput, calls=%fused_computation.18 | convolution fusion | flops 8405385216 | bytes 20697088 | tf_op jit(solution)/shard_map/dot_general | solution.py:73
  91.1 1.3 log-plus-one_bitcast_fusion
  92.4 1.0 copy.34
  93.4 1.1 select_reduce_fusion.1
  94.5 14.1 %select_reduce_fusion = f32[8,1000]{0,1:T(8,128)S(1)} fusion(f32[8,128,1000]{1,0,2:T(8,128)S(1)} %bitcast.52, f32[8,1000]{0,1:T(8,128)S(1)} %select_reduce_fusion.1, pred[8,128]{1,0:T(8,128)(4,1)S(1)} %get-tuple-element.16), kind=kLoop, calls=%fused_computation.15 | loop fusion | flops 4088000 | bytes 4161024 | tf_op jit(solution)/shard_map/reduce_sum | solution.py:46
  108.6 0.2 copy.30
  108.8 0.2 copy.29
  109.0 34.6 %all_gather.13 = f32[64,1000]{1,0:T(8,128)S(1)} all-gather(f32[8,1000]{1,0:T(8,128)S(1)} %multiply_add_fusion), channel_id=1, replica_groups=mesh['dp'=8,'vocab'=16] {'dp'}, dimensions={0}, use_global_device_ids=true | all-gather | bytes 288000 | tf_op jit(solution)/shard_map/all_gather | solution.py:78
  143.6 0.6 broadcast_multiply_fusion
  144.3 0.2 convolution_multiply_fusion.2
  144.6 27.7 %psum.28 = f32[16,48]{1,0:T(8,128)S(1)} all-reduce(f32[16,48]{1,0:T(8,128)S(1)} %convolution_multiply_fusion.2), channel_id=1, replica_groups=mesh['dp'=8,'vocab'=16] {'vocab'}, use_global_device_ids=true, to_apply=%region_3.4 | all-reduce | flops 768 | bytes 6144 | tf_op jit(solution)/shard_map/psum | solution.py:91
  172.3 0.1 reduce_max.19
  172.4 0.2 select_reduce_fusion.3
  172.5 0.2 fusion.19
  172.7 0.6 fusion.25
  173.3 0.1 select_reduce_fusion.2
  173.4 0.1 select_subtract_fusion
  173.5 0.2 convolution_multiply_fusion.1
  173.7 0.3 convolution_multiply_fusion
  174.1 0.2 copy.32
  174.3 1.1 mul.174
  175.4 1.1 sub.45
  176.5 1.1 div.79
  177.7 4.0 %fusion.5 = bf16[1024,1000]{0,1:T(8,128)(2,1)S(1)} fusion(f32[125,8,8,128]{3,2,1,0:T(8,128)S(1)} %bitcast.55, f32[125,8,8,128]{3,2,1,0:T(8,128)S(1)} %bitcast.54, f32[125,8,8,128]{3,2,1,0:T(8,128)S(1)} %bitcast.53, f32[1024,1000]{0,1:T(8,128)S(1)} %copy-done.1, pred[1024]{0:T(1024)(128)(4,1)S(1)} %get-tuple-element.15), kind=kLoop, calls=%fused_computation.10 | loop fusion | flops 12288000 | bytes 18433024 | tf_op jit(solution)/shard_map/convert_element_type | solution.py:54
  181.6 11.4 %convolution_convert_fusion = bf16[1024,4096]{1,0:T(8,128)(2,1)} fusion(bf16[1024,1000]{0,1:T(8,128)(2,1)S(1)} %fusion.5, bf16[4096,1000]{0,1:T(8,128)(2,1)S(1)} %bitcast.61), kind=kOutput, calls=%fused_computation.5 | convolution fusion | flops 8392802304 | bytes 18628608 | tf_op jit(solution)/shard_map/dot_general | solution.py:111
  193.0 0.3 reduce-scatter.5.cloned.1.call-start
  193.3 15.5 %convolution_convert_fusion.1 = bf16[4096,1000]{0,1:T(8,128)(2,1)} fusion(bf16[1024,1000]{0,1:T(8,128)(2,1)S(1)} %fusion.5, bf16[1024,4096]{1,0:T(8,128)(2,1)} %all-gather.3.cloned.1.call-done, f32[4096]{0:T(1024)S(1)} %copy-done.4, f32[1024]{0:T(1024)S(1)} %add_rsqrt_fusion), kind=kOutput, calls=%fused_computation.6 | convolution fusion | flops 8409481216 | bytes 18649088 | tf_op jit(solution)/shard_map/dot_general | solution.py:104
  208.8 0.1 dynamic_slice.11
  208.9 0.6 subtract_reduce_fusion
  210.8 54.8 %reduce-scatter.3.cloned.1.call-done = bf16[1024,256]{1,0:T(8,128)(2,1)} async-done(((bf16[1024,4096]{1,0:T(8,128)(2,1)}), bf16[1024,256]{1,0:T(8,128)(2,1)}) %reduce-scatter.3.cloned.1.call-update) | async-done | bytes 524304 | tf_op jit(solution)/shard_map/reduce_scatter | solution.py:114
  265.6 1.6 fusion.17
  267.2 29.2 %all-reduce.1 = (f32[]{:T(128)}, f32[1024]{0:T(1024)S(1)}) all-reduce(f32[]{:T(128)} %get-tuple-element.13, f32[1024]{0:T(1024)S(1)} %get-tuple-element.5), channel_id=1, replica_groups=mesh['dp'=8,'vocab'=16] {'vocab'}, use_global_device_ids=true, to_apply=%region_12.13 | all-reduce | flops 1025 | bytes 8200 | tf_op jit(solution)/shard_map/psum | solution.py:91
  297.1 24.7 %psum.31 = f32[256]{0:T(256)} all-reduce(f32[256]{0:T(256)S(1)} %get-tuple-element.4), channel_id=1, replica_groups=mesh['dp'=8,'vocab'=16] {'dp'}, use_global_device_ids=true, to_apply=%region_20.21 | all-reduce | flops 256 | bytes 2048 | tf_op jit(solution)/shard_map/psum | solution.py:119
  321.8 0.6 pad_maximum_fusion
  322.3 2.2 fusion.16
  324.6 58.7 %reduce-scatter.5.cloned.1.call-done = bf16[512,1000]{0,1:T(8,128)(2,1)} async-done(((bf16[4096,1000]{0,1:T(8,128)(2,1)}), bf16[512,1000]{0,1:T(8,128)(2,1)}) %reduce-scatter.5.cloned.1.call-update) | async-done | bytes 1024016 | tf_op jit(solution)/shard_map/reduce_scatter | solution.py:103
  (26 shorter events, 0.3 us)
Async XLA Ops:
  7.2 66.1 %all-gather.3.cloned.1.call-start = ((), (), s32[]{:S(2)}) async-start(), calls=%async_computation.2 | async-start | bytes 8912896 | tf_op jit(solution)/shard_map/all_gather | solution.py:70
  7.2 71.3 %copy-start.4 = (f32[4096]{0:T(1024)S(1)}, f32[4096]{0:T(1024)}, u32[]{:S(2)}) copy-start(f32[4096]{0:T(1024)} %param.7) | copy-start | bytes 49156
  7.9 257.7 %reduce-scatter.3.cloned.1.call-start = ((), (), s32[]{:S(2)}) async-start(), calls=%async_computation.3 | async-start | bytes 8912896 | tf_op jit(solution)/shard_map/reduce_scatter | solution.py:114
  73.3 5.8 %copy-start.2 = (bf16[1024,4096]{1,0:T(8,128)(2,1)S(1)}, bf16[1024,4096]{1,0:T(8,128)(2,1)}, u32[]{:S(2)}) copy-start(bf16[1024,4096]{1,0:T(8,128)(2,1)} %all-gather.3.cloned.1.call-done) | copy-start | bytes 25165828
  91.1 2.3 copy-start
  175.4 2.3 copy-start.1
  176.5 5.1 %slice-start = ((s8[8192000]{0:T(1024)(128)(4,1)}), s8[4194304]{0:T(1024)(128)(4,1)S(1)}, s32[]{:S(2)}) async-start(s8[8192000]{0:T(1024)(128)(4,1)} %bitcast.60), calls=%async_computation.5 | async-start | bytes 8388608
  177.6 4.0 %slice-start.1 = ((s8[8192000]{0:T(1024)(128)(4,1)}), s8[3997696]{0:T(1024)(128)(4,1)S(1)}, s32[]{:S(2)}) async-start(s8[8192000]{0:T(1024)(128)(4,1)} %bitcast.60), calls=%async_computation.6 | async-start | bytes 7995392
  193.0 190.2 %reduce-scatter.5.cloned.1.call-start = ((), (), s32[]{:S(2)}) async-start(), calls=%async_computation.4 | async-start | bytes 9216000 | tf_op jit(solution)/shard_map/reduce_scatter | solution.py:103
  208.8 56.8 %copy-start.3 = (bf16[1024,256]{1,0:T(8,128)(2,1)S(1)}, bf16[1024,256]{1,0:T(8,128)(2,1)}, u32[]{:S(2)}) copy-start(bf16[1024,256]{1,0:T(8,128)(2,1)} %param.6) | copy-start | bytes 1572868
Sparse Core Ops, SparseCore 0:
  9.6 63.6 all-gather.2
  193.2 72.3 reduce-scatter.2
  270.1 113.0 reduce-scatter.4
where the time goes:
time: 390 us
  blocking collectives  148 us (38%)
  waiting for transfers between devices  144 us (37%)
  matrix products  39.6 us (10%)
  other arithmetic  33.3 us (9%)
  between operations  16.6 us (4%)
  local copies, waits for them, and re-layouts  7.79 us (2%)
    reduce_scatter x1, waiting for transfers between devices, shards(): lax.psum_scatter(lax.dot_general(normed, local_grad, (((0,), (0,)), ((),...  58.7 us
    psum x2, blocking collectives, shards(): scores, flops_total = lax.psum((part_scores, part_flops), 'vocab')  56.9 us
    reduce_scatter x1, waiting for transfers between devices, shards(): lax.psum_scatter(partial_grad.astype(jnp.bfloat16), 'vocab', scatter_dime...  54.8 us
    all_gather x1, blocking collectives, shards(): lax.all_gather(pooled, 'dp', axis=0, tiled=True)  34.6 us
    all_gather x1, waiting for transfers between devices, shards(): lax.all_gather(hidden, 'vocab', axis=1, tiled=True).astype(jnp.float32)  30 us
    psum x1, blocking collectives, shards(): gain_grad = lax.psum(jnp.sum(normed_grad * unit_local, axis=0), 'dp')  24.7 us
    all_gather x1, blocking collectives, shards(): lax.all_gather(negatives, 'dp', axis=0, tiled=True)  23.9 us
    dot_general x1, matrix products, shards(): lax.dot_general(normed, local_grad, (((0,), (0,)), ((), ())), preferred_e...  15.5 us
  transfers between devices with their start and end apart: 3, of which 3 were waited for; matrix products, arithmetic and copies ran while one was open for 6% of the time, Pallas kernels for 0%

commit v1 on v0

v1 whole, which is shorter than its diff:
```python
import functools
import math

import jax
import jax.numpy as jnp
from jax import lax
from jax.experimental import pallas as pl
from jax.experimental.pallas import tpu as pltpu
from jax.sharding import Mesh, PartitionSpec as P

VOCAB = 16000
D = 4096
epsilon = 1e-05
sharpness = 80.0
flops_weight = 0.01

TOK = 1024
SEQ = 8
LEN = 128
TERMS = 1000
BLK = 256
ROWS_A = 640
ROWS_B = TERMS - ROWS_A
HALF = TOK // 2
PER = 2
SHORT = 8
SCORE_SCALE = 4.0 / math.sqrt(VOCAB)
COLS = ((0, 256), (256, 512), (512, 768), (768, 1000))
SIZES = {"xh": 2, "y": 4, "xl": 2, "z": 4, "c": 2}
VMEM_LIMIT = 56 * 1024 * 1024
HIGHEST = lax.Precision.HIGHEST

f32, bf16 = jnp.float32, jnp.bfloat16


def shift(x, axis, step):
    n = SIZES[axis]
    return lax.ppermute(x, axis, [(i, (i + step) % n) for i in range(n)])


def swap(x, axis, bits=1):
    return lax.ppermute(x, axis, [(i, i ^ bits) for i in range(SIZES[axis])])


def params(**more):
    return pltpu.CompilerParams(vmem_limit_bytes=VMEM_LIMIT, **more)


def cost(flops, moved):
    return pl.CostEstimate(flops=int(flops / SHORT), bytes_accessed=int(moved / SHORT), transcendentals=0)


def tag(ids, pooled_ref):
    lane = lax.broadcasted_iota(jnp.int32, (1, 24), 1)
    for k in range(SEQ):
        tags = jnp.zeros((1, 24), f32)
        if k < 2:
            tags = jnp.where(lane == 0, ids[8 + k].astype(f32), tags)
            tags = jnp.where(lane == 1, ids[10 + 2 * k].astype(f32), tags)
            tags = jnp.where(lane == 2, ids[11 + 2 * k].astype(f32), tags)
        pooled_ref[k : k + 1, TERMS:] = tags


def pool(lengths, first, acc, ssq, inv_ref, weight_ref, pooled_ref):
    for s in range(acc.shape[0] // LEN):
        k = first + s
        rows = slice(s * LEN, (s + 1) * LEN)
        total = jnp.sum(ssq[rows, :], axis=1, keepdims=True)
        inverse = lax.rsqrt(total / D + epsilon)
        inv_ref[rows, :] = inverse
        count = lengths[k]
        for a, b in COLS:
            logits = acc[rows, a:b] * inverse
            valid = lax.broadcasted_iota(jnp.int32, (LEN, b - a), 0) < count
            held = jnp.where(valid, 1.0 + jnp.maximum(logits, 0.0), 1.0)
            top = jnp.max(held, axis=0, keepdims=True)
            down = 1.0 / top
            r1 = held * down
            r2 = r1 * r1
            r4 = r2 * r2
            r8 = r4 * r4
            r16 = r8 * r8
            r32 = r16 * r16
            r79 = (r32 * r32 * r8) * (r4 * (r2 * r1))
            summed = jnp.sum(jnp.where(valid, r79 * r1, 0.0), axis=0, keepdims=True)
            pooled_ref[pl.ds(k, 1), a:b] = jnp.log(top) + jnp.log(summed) / sharpness
            slope = r79 * (down / summed) * inverse
            weight_ref[rows, a:b] = jnp.where(valid & (logits > 0.0), slope, 0.0).astype(bf16)


def chip_of(ids, far_x, step):
    return (ids[2] ^ far_x) * 4 + ((ids[3] + step) & 3)


def block_at(ids, chip, side):
    return pl.ds(pl.multiple_of((chip * 2 + (ids[4] ^ side)) * BLK, BLK), BLK)


def scaled(weights, gain, ids, chip):
    row = jnp.concatenate([gain[:, block_at(ids, chip, side)] for side in range(2)], axis=1)
    return (weights.astype(f32) * row).astype(bf16)


def folded_squares(lefts):
    squares = 0.0
    for left in lefts:
        value = left.astype(f32)
        square = value * value
        squares = squares + square[:, :128] + square[:, 128:]
    return squares


def forward_kernel(places, first, ids, *refs):
    nb = len(places)
    arrays, (weights, gain), refs = refs[: 2 * nb], refs[2 * nb : 2 * nb + 2], refs[2 * nb + 2 :]
    if not first:
        (acc_in, ssq_in, _), refs = refs[:3], refs[3:]
    acc, ssq, kept, held, w_sem, x_sem = refs
    chips = [chip_of(ids, *place) for place in places]
    loads, saves = [], []
    for j in range(nb):
        for side in range(2):
            at = held.at[j, :, side * BLK : (side + 1) * BLK]
            loads.append(pltpu.make_async_copy(weights.at[:, block_at(ids, chips[j], side)], at, w_sem.at[j, side]))
            loads[-1].start()
    for j in range(nb):
        for side in range(2):
            saves.append(pltpu.make_async_copy(arrays[2 * j + side], kept.at[chips[j], side], x_sem.at[j, side]))
            saves[-1].start()
    for j in range(nb):
        loads[2 * j].wait()
        loads[2 * j + 1].wait()
        right = scaled(held[j], gain, ids, chips[j])
        for half in range(2):
            rows = slice(half * HALF, (half + 1) * HALF)
            lefts = [arrays[2 * j + side][rows, :] for side in range(2)]
            squares = folded_squares(lefts)
            product = lax.dot_general(
                jnp.concatenate(lefts, axis=1), right, (((1,), (1,)), ((), ())), preferred_element_type=f32
            )
            if j == 0 and first:
                acc[rows, :] = product
                ssq[rows, :] = squares
            elif j == 0:
                acc[rows, :] = acc_in[rows, :] + product
                ssq[rows, :] = ssq_in[rows, :] + squares
            else:
                acc[rows, :] += product
                ssq[rows, :] += squares
    for copy in saves:
        copy.wait()


SMEM = pl.BlockSpec(memory_space=pltpu.SMEM)
VMEM = pl.BlockSpec(memory_space=pltpu.VMEM)
ANY = pl.BlockSpec(memory_space=pl.ANY)


STATE = [
    jax.ShapeDtypeStruct((TOK, TERMS), f32),
    jax.ShapeDtypeStruct((TOK, 128), f32),
    jax.ShapeDtypeStruct((8, 2, TOK, BLK), bf16),
]


def forward(ids, places, arrays, weights, gain, state=()):
    nb = len(places)
    base = 3 + len(arrays)
    return pl.pallas_call(
        functools.partial(forward_kernel, places, not state),
        out_shape=STATE,
        in_specs=[SMEM] + [VMEM] * len(arrays) + [ANY, VMEM] + [VMEM, VMEM, ANY][: len(state)],
        out_specs=[VMEM, VMEM, ANY],
        scratch_shapes=[
            pltpu.VMEM((nb, TERMS, 2 * BLK), bf16),
            pltpu.SemaphoreType.DMA((nb, 2)),
            pltpu.SemaphoreType.DMA((nb, 2)),
        ],
        input_output_aliases={base + i: i for i in range(len(state))},
        compiler_params=params(),
        cost_estimate=cost(2 * nb * TOK * 512 * TERMS, nb * 3_000_000 + 8_000_000),
        name="forward_part",
    )(ids, *arrays, weights, gain, *state)


STEP = 256


def forward_last_kernel(place, ids, lengths, a0, a1, b0, b1, w0, w1, gain, acc_in, ssq_in, _, *refs):
    product, kept, inv_ref, weight_ref, pooled_ref, acc, right, left, ssq, sem = refs
    k = pl.program_id(0)
    chip = chip_of(ids, *place)

    @pl.when(k == 0)
    def _():
        right[...] = scaled(jnp.concatenate([w0[...], w1[...]], axis=1), gain, ids, chip)
        tag(ids, pooled_ref)

    @pl.when(k < 2)
    def _():
        left[:, :BLK] = a0[...]
        left[:, BLK:] = a1[...]

    @pl.when(k >= 2)
    def _():
        left[:, :BLK] = b0[...]
        left[:, BLK:] = b1[...]

    rows = pl.ds(pl.multiple_of(k * STEP, STEP), STEP)
    saves = []
    for side in range(2):
        source = left.at[:, side * BLK : (side + 1) * BLK]
        saves.append(pltpu.make_async_copy(source, kept.at[chip, side, rows, :], sem.at[side]))
        saves[-1].start()
    ssq[...] = ssq_in[...] + folded_squares([left[:, :BLK], left[:, BLK:]])
    acc[...] = acc_in[...] + lax.dot_general(
        left[...], right[...], (((1,), (1,)), ((), ())), preferred_element_type=f32
    )
    product[...] = acc[...].astype(bf16)
    pool(lengths, k * (STEP // LEN), acc, ssq, inv_ref, weight_ref, pooled_ref)
    for copy in saves:
        copy.wait()


def forward_last(ids, lengths, place, a, b, weights, gain, state):
    whole = lambda k, *s: (0, 0)
    rows = lambda k, *s: (k, 0)
    early = pl.BlockSpec((STEP, BLK), lambda k, *s: (jnp.minimum(k, 1), 0))
    late = pl.BlockSpec((STEP, BLK), lambda k, *s: (jnp.maximum(k - 2, 0), 0))
    sides = [
        pl.BlockSpec((TERMS, BLK), lambda k, s, n, side=side: (0, chip_of(s, *place) * 2 + (s[4] ^ side)))
        for side in range(2)
    ]
    return pl.pallas_call(
        functools.partial(forward_last_kernel, place),
        out_shape=[
            jax.ShapeDtypeStruct((TOK, TERMS), bf16),
            STATE[2],
            jax.ShapeDtypeStruct((TOK, 1), f32),
            jax.ShapeDtypeStruct((TOK, TERMS), bf16),
            jax.ShapeDtypeStruct((SEQ, 1024), f32),
        ],
        grid_spec=pltpu.PrefetchScalarGridSpec(
            num_scalar_prefetch=2,
            grid=(TOK // STEP,),
            in_specs=[early, early, late, late, *sides, pl.BlockSpec((1, D), whole)]
            + [pl.BlockSpec((STEP, TERMS), rows), pl.BlockSpec((STEP, 128), rows), ANY],
            out_specs=[
                pl.BlockSpec((STEP, TERMS), rows),
                ANY,
                pl.BlockSpec((STEP, 1), rows),
                pl.BlockSpec((STEP, TERMS), rows),
                pl.BlockSpec((SEQ, 1024), whole),
            ],
            scratch_shapes=[
                pltpu.VMEM((STEP, TERMS), f32),
                pltpu.VMEM((TERMS, 2 * BLK), bf16),
                pltpu.VMEM((STEP, 2 * BLK), bf16),
                pltpu.VMEM((STEP, 128), f32),
                pltpu.SemaphoreType.DMA((2,)),
            ],
        ),
        input_output_aliases={11: 1},
        compiler_params=params(),
        cost_estimate=cost(2 * TOK * 512 * TERMS, 20_000_000),
        name="forward_last",
    )(ids, lengths, *a, *b, weights, weights, gain, *state)


def touch_kernel(*refs):
    pass


def touch(after, *arrays):
    n = len(arrays)
    return pl.pallas_call(
        touch_kernel,
        out_shape=[jax.ShapeDtypeStruct(a.shape, a.dtype) for a in arrays],
        in_specs=[ANY] * (n + 1),
        out_specs=[ANY] * n,
        input_output_aliases={i + 1: i for i in range(n)},
        compiler_params=params(has_side_effects=True),
        cost_estimate=cost(1000, 1000),
        name="touch",
    )(after, *arrays)


def gram_kernel(ids, p0, p1, p2, p3, all_ref, part_ref):
    xh, y = ids[0], ids[1]
    for j, ref in enumerate((p0, p1, p2, p3)):
        for m in range(2):
            at = (xh ^ m) * 4 + (y ^ j)
            all_ref[pl.ds(pl.multiple_of(at * SEQ, SEQ), SEQ), :] = ref[m]
    every = all_ref[:, :TERMS]
    part = lax.dot_general(every, every, (((1,), (1,)), ((), ())), precision=HIGHEST, preferred_element_type=f32)
    mean = jnp.sum(every, axis=0, keepdims=True) / 64.0
    flops = jnp.sum(mean * mean, axis=1, keepdims=True)
    part_ref[...] = jnp.zeros_like(part_ref)
    part_ref[0:64, 0:64] = part
    part_ref[64:72, :] = jnp.broadcast_to(flops, (8, 128))


def gram(ids, groups):
    whole3 = lambda s: (0, 0, 0)
    return pl.pallas_call(
        gram_kernel,
        out_shape=[jax.ShapeDtypeStruct((64, 1024), f32), jax.ShapeDtypeStruct((72, 128), f32)],
        grid_spec=pltpu.PrefetchScalarGridSpec(
            num_scalar_prefetch=1,
            grid=(),
            in_specs=[pl.BlockSpec(memory_space=pltpu.VMEM)] * 4,
            out_specs=[pl.BlockSpec(memory_space=pltpu.VMEM)] * 2,
        ),
        compiler_params=params(),
        name="gram",
    )(ids, *groups)


def contrast(every, part_a, part_b, scaled_ref, losses_ref):
    sums = part_a[...] + part_b[...]
    scores = sums[0:64, :] * SCORE_SCALE
    row = lax.broadcasted_iota(jnp.int32, (64, 128), 0)
    col = lax.broadcasted_iota(jnp.int32, (64, 128), 1)
    is_query = (row & 7) < 2
    is_passage = ((col & 7) >= 2) & (col < 64)
    tags = every[:, TERMS:]

    def hot(at):
        index = tags[:, at : at + 1]
        group = jnp.floor((index + 0.5) * (1.0 / 6.0))
        place = group * 8.0 + 2.0 + (index - 6.0 * group)
        return (col.astype(f32) == place).astype(f32)

    positive, negatives = hot(0), (hot(1), hot(2))
    highest = jnp.max(jnp.where(is_passage, scores, -3e38), axis=1, keepdims=True)
    shifted = jnp.where(is_passage, jnp.exp(jnp.minimum(scores - highest, 0.0)), 0.0)
    denominator = jnp.sum(shifted, axis=1, keepdims=True)
    log_total = highest + jnp.log(denominator)
    positive_score = jnp.sum(scores * positive, axis=1, keepdims=True)
    query_row = is_query[:, 0:1]
    cross = jnp.sum(jnp.where(query_row, log_total - positive_score, 0.0), axis=0, keepdims=True) / 16.0
    grad = (shifted / denominator - positive) / 16.0
    margin = jnp.zeros((1, 1), f32)
    for negative in negatives:
        gap = jnp.sum(scores * negative, axis=1, keepdims=True) - positive_score
        small = jnp.exp(-jnp.abs(gap))
        soft = jnp.maximum(gap, 0.0) + jnp.log(1.0 + small)
        slope = jnp.where(gap >= 0.0, 1.0, small) / (1.0 + small) / 32.0
        margin = margin + jnp.sum(jnp.where(query_row, soft, 0.0), axis=0, keepdims=True) / 32.0
        grad = grad + slope * negative - slope * positive
    grad = jnp.where(is_query, grad, 0.0)
    square = jnp.concatenate([grad, jnp.zeros((64, 128), f32)], axis=0)
    scaled_ref[...] = (square + square.T) * SCORE_SCALE
    flops = sums[64:65, 0:1] * flops_weight
    lane = lax.broadcasted_iota(jnp.int32, (8, 128), 1)
    losses_ref[...] = jnp.where(lane == 0, cross, jnp.where(lane == 1, margin, flops))


def grad_kernel(
    ids, every, part_a, part_b, weight, acc, h_ref, ht_ref, dots, losses_ref, rep, scaled, padded
):
    k = pl.program_id(0)

    @pl.when(k == 0)
    def _():
        contrast(every, part_a, part_b, scaled, losses_ref)
        padded[0:64, :] = every[:, :TERMS]
        padded[64:128, :] = jnp.zeros((64, TERMS), f32)
        at = pl.multiple_of((ids[0] * 4 + ids[1]) * SEQ, SEQ)
        own = scaled[pl.ds(at, SEQ), :]
        mean = jnp.sum(padded[...], axis=0, keepdims=True) / 64.0
        rep[...] = jnp.dot(own, padded[...], precision=HIGHEST, preferred_element_type=f32) + (
            2.0 * flops_weight / 64.0
        ) * mean

    for s in range(PER):
        rows = slice(s * LEN, (s + 1) * LEN)
        folded = jnp.zeros((LEN, 128), f32)
        for a, b in COLS:
            grad = weight[rows, a:b].astype(f32) * rep[pl.ds(k * PER + s, 1), a:b]
            rounded = grad.astype(bf16)
            h_ref[rows, a:b] = rounded
            turned = grad.T.astype(bf16)
            ht_ref[a:b, rows] = turned
            product = rounded.astype(f32) * acc[rows, a:b].astype(f32)
            wide = b - a
            folded = folded + product[:, :128]
            if wide == 256:
                folded = folded + product[:, 128:]
            else:
                folded = folded + jnp.concatenate([product[:, 128:], jnp.zeros((LEN, 256 - wide), f32)], axis=1)
        dots[pl.ds(k * PER + s, 1), :] = jnp.sum(folded.T, axis=0, keepdims=True)


def grads(ids, every, part_a, part_b, weight, acc):
    whole = lambda k, s: (0, 0)
    rows = lambda k, s: (k, 0)
    cols = lambda k, s: (0, k)
    return pl.pallas_call(
        grad_kernel,
        out_shape=[
            jax.ShapeDtypeStruct((TOK, TERMS), bf16),
            jax.ShapeDtypeStruct((TERMS, TOK), bf16),
            jax.ShapeDtypeStruct((SEQ, LEN), f32),
            jax.ShapeDtypeStruct((8, 128), f32),
        ],
        grid_spec=pltpu.PrefetchScalarGridSpec(
            num_scalar_prefetch=1,
            grid=(SEQ // PER,),
            in_specs=[
                pl.BlockSpec((64, 1024), whole),
                pl.BlockSpec((72, 128), whole),
                pl.BlockSpec((72, 128), whole),
                pl.BlockSpec((PER * LEN, TERMS), rows),
                pl.BlockSpec((PER * LEN, TERMS), rows),
            ],
            out_specs=[
                pl.BlockSpec((PER * LEN, TERMS), rows),
                pl.BlockSpec((TERMS, PER * LEN), cols),
                pl.BlockSpec((SEQ, LEN), whole),
                pl.BlockSpec((8, 128), whole),
            ],
            scratch_shapes=[pltpu.VMEM((SEQ, TERMS), f32), pltpu.VMEM((128, 128), f32), pltpu.VMEM((128, TERMS), f32)],
        ),
        compiler_params=params(),
        cost_estimate=cost(20 * TOK * TERMS, 12_000_000),
        name="logit_grad",
    )(ids, every, part_a, part_b, weight, acc)


def head_kernel(ids, _, ht, x, gain, a00, a01, a10, a11, keep, send):
    n = pl.program_id(0)
    block = jnp.concatenate([x[0, 0], x[0, 1]], axis=1)
    chip = head_chip(ids, n)
    row = jnp.concatenate([gain[:, block_at(ids, chip, side)] for side in range(2)], axis=1)
    total = (jnp.dot(ht[...], block, preferred_element_type=f32) * row).astype(bf16)
    sides = [total[:, :BLK], total[:, BLK:]]
    for when, outs in ((n < 2, (a00, a01)), (n >= 2, (a10, a11))):

        @pl.when(when)
        def _(outs=outs):
            for side in range(2):
                outs[side][0] = sides[side][:ROWS_A]

    for j, out in enumerate((keep, send)):

        @pl.when((n & 1) == j)
        def _(out=out):
            for side in range(2):
                out[0, side] = sides[side][ROWS_A:]


def head_chip(ids, n):
    return (ids[0] ^ (n & 1)) * 4 + ((ids[1] + jnp.where(n < 2, ids[14], ids[15])) & 3)


def head_part(ids, steps, ht, x, gain, after):
    ids = jnp.concatenate([ids, jnp.array(steps, jnp.int32)])
    first = pl.BlockSpec((1, ROWS_A, BLK), lambda n, s: (jnp.minimum(n, 1), 0, 0))
    second = pl.BlockSpec((1, ROWS_A, BLK), lambda n, s: (jnp.maximum(n - 2, 0), 0, 0))
    low = pl.BlockSpec((1, 2, ROWS_B, BLK), lambda n, s: (n // 2, 0, 0, 0))
    return pl.pallas_call(
        head_kernel,
        out_shape=[jax.ShapeDtypeStruct((2, ROWS_A, BLK), bf16)] * 4
        + [jax.ShapeDtypeStruct((2, 2, ROWS_B, BLK), bf16)] * 2,
        grid_spec=pltpu.PrefetchScalarGridSpec(
            num_scalar_prefetch=1,
            grid=(4,),
            in_specs=[
                ANY,
                pl.BlockSpec((TERMS, TOK), lambda n, s: (0, 0)),
                pl.BlockSpec((1, 2, TOK, BLK), lambda n, s: (head_chip(s, n), 0, 0, 0)),
                pl.BlockSpec((1, D), lambda n, s: (0, 0)),
            ],
            out_specs=[first, first, second, second, low, low],
        ),
        compiler_params=params(),
        cost_estimate=cost(2 * TERMS * TOK * 2048, 2 * TERMS * TOK + 4096 * (TOK + TERMS)),
        name="head_part",
    )(ids, after, ht, x, gain)


def join_kernel(ids, r0, r1, a0, a1, got, keep, swapped, b1, b2, b3, out):
    for side, r, a in ((0, r0, a0), (1, r1, a1)):
        cols = pl.ds(pl.multiple_of((ids[4] ^ side) * BLK, BLK), BLK)
        out[0:ROWS_A, cols] = (r[0].astype(f32) + a[0].astype(f32) + got[side].astype(f32)).astype(bf16)
        total = keep[1, side].astype(f32) + swapped[1, side].astype(f32)
        for b in (b1, b2, b3):
            total = total + b[side].astype(f32)
        out[ROWS_A:TERMS, cols] = total.astype(bf16)


def join(ids, *parts):
    return pl.pallas_call(
        join_kernel,
        out_shape=jax.ShapeDtypeStruct((TERMS, 2 * BLK), bf16),
        in_specs=[SMEM] + [VMEM] * len(parts),
        out_specs=VMEM,
        compiler_params=params(),
        cost_estimate=cost(1000, 8_000_000),
        name="join",
    )(ids, *parts)


def term_kernel(n_add, ids, _, h, w0, w1, *refs):
    weights = jnp.concatenate([w0[...], w1[...]], axis=1)
    out = refs[n_add]
    for half in range(2):
        rows = slice(half * HALF, (half + 1) * HALF)
        total = jnp.dot(h[rows, :], weights, preferred_element_type=f32)
        for m in range(2):
            share = total[:, m * BLK : (m + 1) * BLK]
            for ref in refs[:n_add]:
                share = share + ref[0, m, rows, :].astype(f32)
            out[0, m, rows, :] = share.astype(bf16)


def term_part(ids, side, h, wt, after, adds=()):
    block = pl.BlockSpec((1, 2, TOK, BLK), lambda j, s: (j, 0, 0, 0))
    sides = [
        pl.BlockSpec((TERMS, BLK), lambda j, s, m=m: (0, ((s[2] ^ m) * 4 + j) * 2 + (s[4] ^ side))) for m in range(2)
    ]
    return pl.pallas_call(
        functools.partial(term_kernel, len(adds)),
        out_shape=jax.ShapeDtypeStruct((4, 2, TOK, BLK), bf16),
        grid_spec=pltpu.PrefetchScalarGridSpec(
            num_scalar_prefetch=1,
            grid=(4,),
            in_specs=[ANY, pl.BlockSpec((TOK, TERMS), lambda j, s: (0, 0)), *sides] + [block] * len(adds),
            out_specs=block,
        ),
        compiler_params=params(),
        cost_estimate=cost(16 * TOK * BLK * TERMS, 2 * TOK * TERMS + 8 * BLK * (2 * TERMS + 4 * TOK)),
        name="term_part",
    )(ids, after, h, wt, wt, *adds)


def gain_kernel(n, x, x_p, out):
    for m, ref in ((0, x), (1, x_p)):
        sums = jnp.zeros((8, BLK), f32)
        for k in range(SEQ):
            rows = slice(k * LEN, (k + 1) * LEN)
            sums = sums + jnp.sum((n[m, rows, :].astype(f32) * ref[rows, :].astype(f32)).reshape(LEN // 8, 8, BLK), axis=0)
        out[m] = jnp.sum(sums, axis=0, keepdims=True)


def gain_part(n, x, x_p):
    return pl.pallas_call(
        gain_kernel,
        out_shape=jax.ShapeDtypeStruct((2, 1, BLK), f32),
        in_specs=[VMEM] * 3,
        out_specs=VMEM,
        compiler_params=params(),
        cost_estimate=cost(1_000_000, 2_000_000),
        name="gain_part",
    )(n, x, x_p)


def final_kernel(ids, n_ref, got, x_ref, gain, inv_ref, da, db, out):
    g = gain[:, block_at(ids, ids[2] * 4 + ids[3], 0)]
    lines = (da[...] + db[...]) / D
    for k in range(SEQ):
        rows = slice(k * LEN, (k + 1) * LEN)
        grad = n_ref[0, rows, :].astype(f32) + got[rows, :].astype(f32)
        values = x_ref[rows, :].astype(f32)
        column = jnp.broadcast_to(lines[k : k + 1, :], (LEN, LEN)).T[:, 0:1]
        inverse = inv_ref[rows, :]
        out[rows, :] = (grad * g - values * (inverse * inverse * column)).astype(bf16)


def final(ids, n, got, x, gain, inv, da, db):
    return pl.pallas_call(
        final_kernel,
        out_shape=jax.ShapeDtypeStruct((TOK, BLK), bf16),
        in_specs=[SMEM] + [VMEM] * 7,
        out_specs=VMEM,
        compiler_params=params(),
        cost_estimate=cost(1_000_000, 2_000_000),
        name="hidden_grad",
    )(ids, n, got, x, gain, inv, da, db)


def shards(hidden, norm_gain, head_weight, lengths, positives, negatives):
    xh, y, xl, z, c = (lax.axis_index(a).astype(jnp.int32) for a in ("xh", "y", "xl", "z", "c"))
    nil = jnp.int32(0)
    ids = jnp.concatenate([jnp.stack([xh, y, xl, z, c, nil, nil, nil]), positives, negatives.reshape(-1)])
    wt = head_weight.T
    gain = norm_gain.reshape(1, D)

    z_m, z_p, x_p = shift(hidden, "z", 1), shift(hidden, "z", -1), swap(hidden, "xl")
    own_c = swap(hidden, "c")
    z_m_c, z_p_c, x_p_c = (swap(a, "c") for a in (z_m, z_p, x_p))
    far, xz_p, xz_m = shift(z_m, "z", 1), shift(x_p, "z", -1), swap(z_m, "xl")
    state = forward(ids, [(0, 0), (0, -1), (1, 0)], [hidden, own_c, z_m, z_m_c, x_p, x_p_c], wt, gain)
    far, xz_p, xz_m = touch(state[1], far, xz_p, xz_m)
    far_c, xz_p_c, xz_m_c = (swap(a, "c") for a in (far, xz_p, xz_m))
    last_a, last_b = shift(xz_m[:HALF], "z", 1), shift(xz_p[HALF:], "z", -1)
    state = forward(
        ids,
        [(0, 1), (0, 2), (1, 1), (1, -1)],
        [z_p, z_p_c, far, far_c, xz_p, xz_p_c, xz_m, xz_m_c],
        wt,
        gain,
        state,
    )
    last_a, last_b = touch(state[1], last_a, last_b)
    last_a_c, last_b_c = swap(last_a, "c"), swap(last_b, "c")
    acc, x, inv, weight, pooled = forward_last(
        ids, lengths, (1, 2), (last_a, last_a_c), (last_b, last_b_c), wt, gain, state
    )

    pair = jnp.stack([pooled, swap(pooled, "xh")])
    every, part = gram(ids, [pair] + [swap(pair, "y", j) for j in (1, 2, 3)])
    part = part + swap(part, "c")
    part = (part + swap(part, "z", 1)) + (swap(part, "z", 2) + swap(part, "z", 3))
    h, ht, dots, losses = grads(ids, every, part, swap(part, "xl"), weight, acc)

    crossing = term_part(ids, 1, h, wt, ht)
    a3_own, a3_oth, a1_own, a1_oth, keep_31, send_31 = head_part(ids, (3, 1), ht, x, gain, crossing)
    crossed = swap(crossing, "c")
    term = term_part(ids, 0, h, wt, a3_own, (crossed,))
    a2_own, a2_oth, a0_own, a0_oth, keep_20, send_20 = head_part(ids, (2, 0), ht, x, gain, term)
    summed = lax.psum_scatter(term, "z", scatter_dimension=0, tiled=False)
    partial = gain_part(summed, hidden, x_p)
    gain_grad = partial[0] + swap(partial[1], "xl")
    gain_grad = gain_grad + swap(gain_grad, "xh")
    gain_grad = (gain_grad + swap(gain_grad, "y", 1)) + (swap(gain_grad, "y", 2) + swap(gain_grad, "y", 3))
    got_term = swap(summed[1], "xl")

    own, oth = shift(a3_own, "y", 1), shift(a1_oth, "y", -1)
    swapped_31, swapped_20 = swap(send_31, "xh"), swap(send_20, "xh")
    own, oth = shift(own + a2_own, "y", 1), shift(oth + a2_oth, "y", -1)
    a1_own, a3_oth = touch(swapped_31, a1_own, a3_oth)
    own, oth = shift(own + a1_own, "y", 1), shift(oth + a3_oth, "y", -1)
    got = swap(jnp.stack([own[1] + a0_own[1], oth[1] + a0_oth[1]]), "xh")
    low = [
        shift(keep_31[1] + swapped_31[1], "y", 1),
        shift(keep_20[0] + swapped_20[0], "y", 2),
        shift(keep_31[0] + swapped_31[0], "y", 3),
    ]
    head_t = join(ids, own, oth, a0_own, a0_oth, got, keep_20, swapped_20, *low)

    dots = dots + swap(dots, "c")
    dots = (dots + swap(dots, "z", 1)) + (swap(dots, "z", 2) + swap(dots, "z", 3))
    hidden_grad = final(ids, summed, got_term, hidden, gain, inv, dots, swap(dots, "xl"))
    return losses[0, :3], hidden_grad, head_t.T, gain_grad[0]


def solution(mesh):
    fine = Mesh(mesh.devices.reshape(2, 4, 2, 4, 2), ("xh", "y", "xl", "z", "c"))
    dp, vocab = ("xh", "y"), ("xl", "z", "c")
    in_specs = (P(dp, vocab), P(), P(None, vocab), P(dp), P(dp), P(dp, None))
    out_specs = (P(), P(dp, vocab), P(dp, vocab), P(vocab))
    return jax.shard_map(shards, mesh=fine, in_specs=in_specs, out_specs=out_specs, check_vma=False)
```

time: 390 us -> 266 us (0.68)
  blocking collectives: 148 us -> 0 us
  Pallas kernels: 0 us -> 92.5 us
  waiting for transfers between devices: 144 us -> 67.8 us
  starting transfers between devices: 0.34 us -> 63.5 us
  matrix products: 39.6 us -> 0 us
  other arithmetic: 33.3 us -> 8.24 us
  local copies, waits for them, and re-layouts: 7.79 us -> 17.5 us
    reduce_scatter x2 -> x1, waiting for transfers between devices: 114 us -> 0.02 us  [shards(): summed = lax.psum_scatter(term, 'z', scatter_dimension=0, tiled=False)]
    pallas_call x0 -> x15, Pallas kernels: none -> 92.5 us  [the longest x2 23.3 us: forward(): pl.pallas_call(functools.partial(forward_kernel, places, not state), out_...]
    psum x3 -> x0, blocking collectives: 81.6 us -> none  [the longest x2 56.9 us: shards(): scores, flops_total = lax.psum((part_scores, part_flops), 'vocab')]
    ppermute x0 -> x50, waiting for transfers between devices: none -> 67.7 us  [the longest x15 35.5 us: shift(): return lax.ppermute(x, axis, [(i, (i + step) % n) for i in range(n)])]
    ppermute x0 -> x50, starting transfers between devices: none -> 63.4 us  [the longest x35 39.2 us: swap(): return lax.ppermute(x, axis, [(i, i ^ bits) for i in range(SIZES[axis])])]
    all_gather x2 -> x0, blocking collectives: 58.5 us -> none  [the longest x1 34.6 us: shards(): lax.all_gather(pooled, 'dp', axis=0, tiled=True)]
    dot_general x6 -> x0, matrix products: 39.6 us -> none  [the longest x1 15.5 us: shards(): lax.dot_general(normed, local_grad, (((0,), (0,)), ((), ())), preferred_e...]
    all_gather x1 -> x0, waiting for transfers between devices: 30 us -> none  [shards(): lax.all_gather(hidden, 'vocab', axis=1, tiled=True).astype(jnp.float32)]
  transfers between devices with their start and end apart: 3 -> 51, of which waited for: 3 -> 17; matrix products, arithmetic and copies ran while one was open for 6% -> 6% of each run, Pallas kernels for 0% -> 19%
where the time goes in v1:
time: 266 us; the launch traced here: 264 us
  Pallas kernels  92.5 us (35%)
  waiting for transfers between devices  67.8 us (25%)
  starting transfers between devices  63.5 us (24%)
  local copies, waits for them, and re-layouts  17.5 us (7%)
  between operations  14.5 us (5%)
  other arithmetic  8.24 us (3%)
    ppermute x35, starting transfers between devices, swap(): return lax.ppermute(x, axis, [(i, i ^ bits) for i in range(SIZES[axis])])  39.2 us
    ppermute x15, waiting for transfers between devices, shift(): return lax.ppermute(x, axis, [(i, (i + step) % n) for i in range(n)])  35.5 us
    ppermute x35, waiting for transfers between devices, swap(): return lax.ppermute(x, axis, [(i, i ^ bits) for i in range(SIZES[axis])])  32.2 us
    ppermute x15, starting transfers between devices, shift(): return lax.ppermute(x, axis, [(i, (i + step) % n) for i in range(n)])  24.3 us
    pallas_call x2, Pallas kernels, forward(): pl.pallas_call(functools.partial(forward_kernel, places, not state), out_...  23.3 us
    pallas_call x2, Pallas kernels, head_part(): pl.pallas_call(head_kernel, out_shape=[jax.ShapeDtypeStruct((2, ROWS_A, B...  19.3 us
    pallas_call x2, Pallas kernels, term_part(): pl.pallas_call(functools.partial(term_kernel, len(adds)), out_shape=jax.S...  19.1 us
    pallas_call x1, Pallas kernels, forward_last(): pl.pallas_call(functools.partial(forward_last_kernel, place), out_shape=[...  12.4 us
  transfers between devices with their start and end apart: 51, of which 17 were waited for; matrix products, arithmetic and copies ran while one was open for 6% of the time, Pallas kernels for 19%

profile of v1, /device:TPU:0, one launch (start us, length us, event | category | flops | bytes accessed | tf_op | source)
XLA Modules:
  0.0 264.0 jit_solution(4725744139637954366)
XLA Ops:
  7.2 2.1 collective-permute-start.3
  9.3 1.5 collective-permute-start.5
  10.8 2.2 collective-permute-start
  13.0 10.7 %collective-permute-done.3.refs_2_ = bf16[1024,256]{1,0:T(8,128)(2,1)} collective-permute-done((bf16[1024,256]{1,0:T(8,128)(2,1)}, bf16[1024,256]{1,0:T(8,128)(2,1)}, u32[]{:S(2)}, u32[]{:S(2)}) %collective-permute-start.3) | collective-permute-done | bytes 524320 | tf_op jit(solution)/shard_map/ppermute | solution.py:38
  24.8 2.6 collective-permute-start.8
  27.4 1.5 collective-permute-start.9
  31.7 10.1 %forward_part.2 = (f32[1024,1000]{1,0:T(8,128)}, f32[1024,128]{1,0:T(8,128)}, bf16[8,2,1024,256]{3,2,1,0:T(8,128)(2,1)}) custom-call(s32[14]{0:T(128)} %concatenate.11.ids, bf16[1024,256]{1,0:T(8,128)(2,1)} %x.1, bf16[1024,256]{1,0:T(8,128)(2,1)} %copy-done.19, bf16[1024,256]{1,0:T(8,128)(2,1)} %collective-permute-done.3.refs_2_, ...), custom_call_target="tpu_custom_call" | custom-call | flops 393216000 | bytes 2125000 | tf_op jit(solution)/shard_map/forward_part/pallas_call | solution.py:169
  46.1 3.2 %collective-permute-start.14 = (bf16[512,256]{1,0:T(8,128)(2,1)S(1)}, bf16[512,256]{1,0:T(8,128)(2,1)S(1)}, u32[]{:S(2)}, u32[]{:S(2)}) collective-permute-start(bf16[512,256]{1,0:T(8,128)(2,1)S(1)} %slice.50), channel_id=1, source_target_pairs={{0,6},{2,0},{4,2},{6,4},{1,7},{3,1},{5,3},{7,5},{8,14},{10,8},{12,... | collective-permute-start | bytes 786440 | tf_op jit(solution)/shard_map/ppermute | solution.py:38
  50.4 13.2 %forward_part.3 = (f32[1024,1000]{1,0:T(8,128)}, f32[1024,128]{1,0:T(8,128)}, bf16[8,2,1024,256]{3,2,1,0:T(8,128)(2,1)}) custom-call(s32[14]{0:T(128)} %concatenate.11.ids, bf16[1024,256]{1,0:T(8,128)(2,1)} %copy-done.17, bf16[1024,256]{1,0:T(8,128)(2,1)} %copy-done.18, ...), custom_call_target="tpu_custom_call", output_to_operand_aliasing={{0}: (11, {}), {1}: (12, {}), {2}: (13, {})} | custom-call | flops 524288000 | bytes 2500000 | tf_op jit(solution)/shard_map/forward_part/pallas_call | solution.py:169
  67.2 12.4 %forward_last.1 = (bf16[1024,1000]{1,0:T(8,128)(2,1)}, bf16[8,2,1024,256]{3,2,1,0:T(8,128)(2,1)}, f32[1024,1]{1,0:T(8,128)}, bf16[1024,1000]{1,0:T(8,128)(2,1)}, f32[8,1024]{1,0:T(8,128)}) custom-call(s32[14]{0:T(128)} %concatenate.11.ids, s32[8]{0:T(128)} %lengths.1, bf16[512,256]{1,0:T(8,128)(2,1)} %get-tuple-element.47.a0, ...), custom_call_target="tpu_custom_call", output_to_operand_aliasing={{1}: (11, {})} | custom-call | flops 131072000 | bytes 2500000 | tf_op jit(solution)/shard_map/forward_last/pallas_call | solution.py:234
  79.7 2.8 %collective-permute-start.17 = (f32[8,1024]{1,0:T(8,128)}, f32[8,1024]{1,0:T(8,128)S(1)}, u32[]{:S(2)}, u32[]{:S(2)}) collective-permute-start(f32[8,1024]{1,0:T(8,128)} %get-tuple-element.51), channel_id=1, source_target_pairs={{0,64},{64,0},{1,65},{65,1},{2,66},{66,2},{3,67},{67,3},{4,68},{68... | collective-permute-start | bytes 98312 | tf_op jit(solution)/shard_map/ppermute | solution.py:42
  82.5 2.9 %collective-permute-done.17 = f32[8,1024]{1,0:T(8,128)S(1)} collective-permute-done((f32[8,1024]{1,0:T(8,128)}, f32[8,1024]{1,0:T(8,128)S(1)}, u32[]{:S(2)}, u32[]{:S(2)}) %collective-permute-start.17) | collective-permute-done | bytes 32800 | tf_op jit(solution)/shard_map/ppermute | solution.py:42
  86.1 1.6 collective-permute-start.18
  87.7 2.9 %collective-permute-start.19 = (f32[2,8,1024]{2,1,0:T(8,128)S(1)}, f32[2,8,1024]{2,1,0:T(8,128)S(1)}, u32[]{:S(2)}, u32[]{:S(2)}) collective-permute-start(f32[2,8,1024]{2,1,0:T(8,128)S(1)} %pad_maximum_fusion.1.p0), channel_id=1, source_target_pairs={{0,32},{16,48},{32,0},{48,16},{1,33},{17,49},{33,1},{49,17},{2,34}... | collective-permute-start | bytes 196616 | tf_op jit(solution)/shard_map/ppermute | solution.py:42
  90.8 2.8 %collective-permute-done.19.p2 = f32[2,8,1024]{2,1,0:T(8,128)S(1)} collective-permute-done((f32[2,8,1024]{2,1,0:T(8,128)S(1)}, f32[2,8,1024]{2,1,0:T(8,128)S(1)}, u32[]{:S(2)}, u32[]{:S(2)}) %collective-permute-start.19) | collective-permute-done | bytes 65568 | tf_op jit(solution)/shard_map/ppermute | solution.py:42
  93.7 2.4 collective-permute-done.20.p3
  96.7 2.6 gram.1
  99.3 1.4 collective-permute-done.21
  101.5 1.6 collective-permute-start.23
  103.1 3.1 %collective-permute-start.24 = (f32[72,128]{1,0:T(8,128)S(1)}, f32[72,128]{1,0:T(8,128)S(1)}, u32[]{:S(2)}, u32[]{:S(2)}) collective-permute-start(f32[72,128]{1,0:T(8,128)S(1)} %add.79), channel_id=1, source_target_pairs={{0,6},{2,4},{4,2},{6,0},{1,7},{3,5},{5,3},{7,1},{8,14},{10,12},{12... | collective-permute-start | bytes 110600 | tf_op jit(solution)/shard_map/ppermute | solution.py:42
  108.9 3.4 %collective-permute-done.25.part_b = f32[72,128]{1,0:T(8,128)S(1)} collective-permute-done((f32[72,128]{1,0:T(8,128)S(1)}, f32[72,128]{1,0:T(8,128)S(1)}, u32[]{:S(2)}, u32[]{:S(2)}) %collective-permute-start.25) | collective-permute-done | bytes 36896 | tf_op jit(solution)/shard_map/ppermute | solution.py:42
  112.9 6.5 %logit_grad.1 = (bf16[1024,1000]{1,0:T(8,128)(2,1)}, bf16[1000,1024]{1,0:T(8,128)(2,1)}, f32[8,128]{1,0:T(8,128)}, f32[8,128]{1,0:T(8,128)}) custom-call(s32[14]{0:T(128)} %concatenate.11.ids, f32[64,1024]{1,0:T(8,128)} %get-tuple-element.52.every, f32[72,128]{1,0:T(8,128)} %copy-done.31, f32[72,128]{1,0:T(8,128)} %copy-done.35, ...), custom_call_target="tpu_custom_call" | custom-call | flops 2560000 | bytes 1500000 | tf_op jit(solution)/shard_map/logit_grad/pallas_call | solution.py:399
  119.5 9.2 %term_part.2._ = bf16[4,2,1024,256]{3,2,1,0:T(8,128)(2,1)} custom-call(s32[14]{0:T(128)} %concatenate.11.ids, bf16[1000,1024]{1,0:T(8,128)(2,1)} %get-tuple-element.57._.ht, bf16[1024,1000]{1,0:T(8,128)(2,1)} %get-tuple-element.58.h, bf16[1000,4096]{1,0:T(8,128)(2,1)} %bitcast.32, bf16[1000,4096]{1,0:T(8,128)(2,1)} %bitcast.33), custom_call_target="tpu_custom_call" | custom-call | flops 524288000 | bytes 1816576 | tf_op jit(solution)/shard_map/term_part/pallas_call | solution.py:523
  129.3 9.6 %head_part.2 = (bf16[2,640,256]{2,1,0:T(8,128)(2,1)}, bf16[2,640,256]{2,1,0:T(8,128)(2,1)}, bf16[2,640,256]{2,1,0:T(8,128)(2,1)}, bf16[2,640,256]{2,1,0:T(8,128)...) custom-call(s32[16]{0:T(128)} %concatenate.12.ids, bf16[4,2,1024,256]{3,2,1,0:T(8,128)(2,1)} %term_part.2._, ...), custom_call_target="tpu_custom_call" | custom-call | flops 524288000 | bytes 1292288 | tf_op jit(solution)/shard_map/head_part/pallas_call | solution.py:462
  138.9 10.0 %term_part.3._ = bf16[4,2,1024,256]{3,2,1,0:T(8,128)(2,1)} custom-call(s32[14]{0:T(128)} %concatenate.11.ids, bf16[2,640,256]{2,1,0:T(8,128)(2,1)} %get-tuple-element.60._, bf16[1024,1000]{1,0:T(8,128)(2,1)} %get-tuple-element.58.h, bf16[1000,4096]{1,0:T(8,128)(2,1)} %bitcast.34, bf16[1000,4096]{1,0:T(8,128)(2,1)} %bitcast.35, ...), custom_call_target="tpu_custom_call" | custom-call | flops 524288000 | bytes 1816576 | tf_op jit(solution)/shard_map/term_part/pallas_call | solution.py:523
  150.0 3.2 %collective-permute-start.37 = (bf16[2,640,256]{2,1,0:T(8,128)(2,1)}, bf16[2,640,256]{2,1,0:T(8,128)(2,1)S(1)}, u32[]{:S(2)}, u32[]{:S(2)}) collective-permute-start(bf16[2,640,256]{2,1,0:T(8,128)(2,1)} %get-tuple-element.68), channel_id=1, source_target_pairs={{0,48},{16,0},{32,16},{48,32},{1,49},{17,1},{33,17},{49,33},{2,50}... | collective-permute-start | bytes 1966088 | tf_op jit(solution)/shard_map/ppermute | solution.py:38
  153.2 2.7 %collective-permute-start.35 = (bf16[2,2,360,256]{3,2,1,0:T(8,128)(2,1)}, bf16[2,2,360,256]{3,2,1,0:T(8,128)(2,1)S(1)}, u32[]{:S(2)}, u32[]{:S(2)}) collective-permute-start(bf16[2,2,360,256]{3,2,1,0:T(8,128)(2,1)} %get-tuple-element.64), channel_id=1, source_target_pairs={{0,64},{64,0},{1,65},{65,1},{2,66},{66,2},{3,67},{67,3},{4,68},{68... | collective-permute-start | bytes 2211848 | tf_op jit(solution)/shard_map/ppermute | solution.py:42
  156.5 9.7 %head_part.3 = (bf16[2,640,256]{2,1,0:T(8,128)(2,1)}, bf16[2,640,256]{2,1,0:T(8,128)(2,1)}, bf16[2,640,256]{2,1,0:T(8,128)(2,1)}, bf16[2,640,256]{2,1,0:T(8,128)...) custom-call(s32[16]{0:T(128)} %concatenate.13.ids, bf16[4,2,1024,256]{3,2,1,0:T(8,128)(2,1)} %term_part.3._, ...), custom_call_target="tpu_custom_call" | custom-call | flops 524288000 | bytes 1292288 | tf_op jit(solution)/shard_map/head_part/pallas_call | solution.py:462
  166.2 2.1 collective-permute-done.33
  168.3 1.3 add.87
  169.7 1.4 add.89
  171.1 3.2 %collective-permute-start.38 = (bf16[2,640,256]{2,1,0:T(8,128)(2,1)S(1)}, bf16[2,640,256]{2,1,0:T(8,128)(2,1)S(1)}, u32[]{:S(2)}, u32[]{:S(2)}) collective-permute-start(bf16[2,640,256]{2,1,0:T(8,128)(2,1)S(1)} %add.89), channel_id=1, source_target_pairs={{0,48},{16,0},{32,16},{48,32},{1,49},{17,1},{33,17},{49,33},{2,50}... | collective-permute-start | bytes 1966088 | tf_op jit(solution)/shard_map/ppermute | solution.py:38
  174.3 2.7 %collective-permute-start.41 = (bf16[2,2,360,256]{3,2,1,0:T(8,128)(2,1)}, bf16[2,2,360,256]{3,2,1,0:T(8,128)(2,1)S(1)}, u32[]{:S(2)}, u32[]{:S(2)}) collective-permute-start(bf16[2,2,360,256]{3,2,1,0:T(8,128)(2,1)} %get-tuple-element.74), channel_id=1, source_target_pairs={{0,64},{64,0},{1,65},{65,1},{2,66},{66,2},{3,67},{67,3},{4,68},{68... | collective-permute-start | bytes 2211848 | tf_op jit(solution)/shard_map/ppermute | solution.py:42
  177.9 9.4 %collective-permute-done.34 = bf16[2,640,256]{2,1,0:T(8,128)(2,1)S(1)} collective-permute-done((bf16[2,640,256]{2,1,0:T(8,128)(2,1)S(1)}, bf16[2,640,256]{2,1,0:T(8,128)(2,1)S(1)}, u32[]{:S(2)}, u32[]{:S(2)}) %collective-permute-start.34) | collective-permute-done | bytes 655392 | tf_op jit(solution)/shard_map/ppermute | solution.py:38
  190.6 3.9 %collective-permute-start.30 = (f32[8,128]{1,0:T(8,128)S(1)}, f32[8,128]{1,0:T(8,128)S(1)}, u32[]{:S(2)}, u32[]{:S(2)}) collective-permute-start(f32[8,128]{1,0:T(8,128)S(1)} %add.83), channel_id=1, source_target_pairs={{0,4},{2,6},{4,0},{6,2},{1,5},{3,7},{5,1},{7,3},{8,12},{10,14},{12... | collective-permute-start | bytes 12296 | tf_op jit(solution)/shard_map/ppermute | solution.py:42
  194.5 1.3 add.90
  195.8 3.2 %collective-permute-start.39 = (bf16[2,640,256]{2,1,0:T(8,128)(2,1)S(1)}, bf16[2,640,256]{2,1,0:T(8,128)(2,1)S(1)}, u32[]{:S(2)}, u32[]{:S(2)}) collective-permute-start(bf16[2,640,256]{2,1,0:T(8,128)(2,1)S(1)} %add.90), channel_id=1, source_target_pairs={{0,48},{16,0},{32,16},{48,32},{1,49},{17,1},{33,17},{49,33},{2,50}... | collective-permute-start | bytes 1966088 | tf_op jit(solution)/shard_map/ppermute | solution.py:38
  199.3 6.2 %collective-permute-done.36.r0 = bf16[2,640,256]{2,1,0:T(8,128)(2,1)S(1)} collective-permute-done((bf16[2,640,256]{2,1,0:T(8,128)(2,1)S(1)}, bf16[2,640,256]{2,1,0:T(8,128)(2,1)S(1)}, u32[]{:S(2)}, u32[]{:S(2)}) %collective-permute-start.36) | collective-permute-done | bytes 655392 | tf_op jit(solution)/shard_map/ppermute | solution.py:38
  205.6 7.2 %collective-permute-done.39.r1 = bf16[2,640,256]{2,1,0:T(8,128)(2,1)S(1)} collective-permute-done((bf16[2,640,256]{2,1,0:T(8,128)(2,1)S(1)}, bf16[2,640,256]{2,1,0:T(8,128)(2,1)S(1)}, u32[]{:S(2)}, u32[]{:S(2)}) %collective-permute-start.39) | collective-permute-done | bytes 655392 | tf_op jit(solution)/shard_map/ppermute | solution.py:38
  213.7 2.2 gain_part.1
  217.1 3.0 %collective-permute-done.45 = f32[1,256]{1,0:T(1,128)S(1)} collective-permute-done((f32[1,256]{1,0:T(1,128)S(1)}, f32[1,256]{1,0:T(1,128)S(1)}, u32[]{:S(2)}, u32[]{:S(2)}) %collective-permute-start.45) | collective-permute-done | bytes 1056 | tf_op jit(solution)/shard_map/ppermute | solution.py:42
  220.1 3.7 %collective-permute-start.44 = (bf16[2,360,256]{2,1,0:T(8,128)(2,1)S(1)}, bf16[2,360,256]{2,1,0:T(8,128)(2,1)S(1)}, u32[]{:S(2)}, u32[]{:S(2)}) collective-permute-start(bf16[2,360,256]{2,1,0:T(8,128)(2,1)S(1)} %get-tuple-element.76), channel_id=1, source_target_pairs={{0,48},{16,0},{32,16},{48,32},{1,49},{17,1},{33,17},{49,33},{2,50}... | collective-permute-start | bytes 1105928 | tf_op jit(solution)/shard_map/ppermute | solution.py:38
  224.5 2.8 %collective-permute-start.40 = (bf16[2,640,256]{2,1,0:T(8,128)(2,1)S(1)}, bf16[2,640,256]{2,1,0:T(8,128)(2,1)S(1)}, u32[]{:S(2)}, u32[]{:S(2)}) collective-permute-start(bf16[2,640,256]{2,1,0:T(8,128)(2,1)S(1)} %pad_maximum_fusion), channel_id=1, source_target_pairs={{0,64},{64,0},{1,65},{65,1},{2,66},{66,2},{3,67},{67,3},{4,68},{68... | collective-permute-start | bytes 1966088 | tf_op jit(solution)/shard_map/ppermute | solution.py:42
  229.2 11.4 %collective-permute-done.46 = f32[1,256]{1,0:T(1,128)S(1)} collective-permute-done((f32[1,256]{1,0:T(1,128)S(1)}, f32[1,256]{1,0:T(1,128)S(1)}, u32[]{:S(2)}, u32[]{:S(2)}) %collective-permute-start.46) | collective-permute-done | bytes 1056 | tf_op jit(solution)/shard_map/ppermute | solution.py:42
  242.6 2.8 %collective-permute-start.48 = (f32[1,256]{1,0:T(1,128)S(1)}, f32[1,256]{1,0:T(1,128)S(1)}, u32[]{:S(2)}, u32[]{:S(2)}) collective-permute-start(f32[1,256]{1,0:T(1,128)S(1)} %add.100), channel_id=1, source_target_pairs={{0,32},{16,48},{32,0},{48,16},{1,33},{17,49},{33,1},{49,17},{2,34}... | collective-permute-start | bytes 3080 | tf_op jit(solution)/shard_map/ppermute | solution.py:42
  246.6 2.1 collective-permute-start.32
  248.7 4.1 %join.1 = bf16[1000,512]{1,0:T(8,128)(2,1)} custom-call(s32[14]{0:T(128)} %concatenate.11.ids, bf16[2,640,256]{2,1,0:T(8,128)(2,1)} %copy-done.10, bf16[2,640,256]{2,1,0:T(8,128)(2,1)} %copy-done.11, bf16[2,640,256]{2,1,0:T(8,128)(2,1)} %get-tuple-element.71.a0, bf16[2,640,256]{2,1,0:T(8,128)(2,1)} %get-tuple-element.72.a1, bf16[2,640,256]{2,1,0:T(8,128)(2,1)} %copy-done.16, ...), custom_call_target="tpu_custom_call" | custom-call | flops 125 | bytes 1000000 | tf_op jit(solution)/shard_map/join/pallas_call | solution.py:494
  254.2 2.9 %hidden_grad.1 = bf16[1024,256]{1,0:T(8,128)(2,1)} custom-call(s32[14]{0:T(128)} %concatenate.11.ids, bf16[2,1024,256]{2,1,0:T(8,128)(2,1)} %bitcast.37, bf16[1024,256]{1,0:T(8,128)(2,1)} %copy-done.24, bf16[1024,256]{1,0:T(8,128)(2,1)} %x.1, f32[1,4096]{1,0:T(1,128)} %bitcast.44, f32[1024,1]{1,0:T(8,128)} %get-tuple-element.61.inv_ref, ...), custom_call_target="tpu_custom_call" | custom-call | flops 125000 | bytes 250000 | tf_op jit(solution)/shard_map/hidden_grad/pallas_call | solution.py:572
  (181 shorter events, 34.7 us)
Async XLA Ops:
  7.2 206.5 %reduce-scatter.2.cloned.1.call-start = ((), (), s32[]{:S(2)}) async-start(), calls=%async_computation.1 | async-start | bytes 5242880 | tf_op jit(solution)/shard_map/reduce_scatter | solution.py:623
  7.2 16.4 %collective-permute-start.3 = (bf16[1024,256]{1,0:T(8,128)(2,1)}, bf16[1024,256]{1,0:T(8,128)(2,1)}, u32[]{:S(2)}, u32[]{:S(2)}) collective-permute-start(bf16[1024,256]{1,0:T(8,128)(2,1)} %x.1), channel_id=1, source_target_pairs={{0,2},{2,4},{4,6},{6,0},{1,3},{3,5},{5,7},{7,1},{8,10},{10,12},{12... | collective-permute-start | bytes 1572872 | tf_op jit(solution)/shard_map/ppermute | solution.py:38
  9.3 14.4 %collective-permute-start.5 = (bf16[1024,256]{1,0:T(8,128)(2,1)}, bf16[1024,256]{1,0:T(8,128)(2,1)S(1)}, u32[]{:S(2)}, u32[]{:S(2)}) collective-permute-start(bf16[1024,256]{1,0:T(8,128)(2,1)} %x.1), channel_id=1, source_target_pairs={{0,8},{8,0},{1,9},{9,1},{2,10},{10,2},{3,11},{11,3},{4,12},{12,4},... | collective-permute-start | bytes 1572872 | tf_op jit(solution)/shard_map/ppermute | solution.py:42
  10.8 14.0 %collective-permute-start.2 = (bf16[1024,256]{1,0:T(8,128)(2,1)}, bf16[1024,256]{1,0:T(8,128)(2,1)S(1)}, u32[]{:S(2)}, u32[]{:S(2)}) collective-permute-start(bf16[1024,256]{1,0:T(8,128)(2,1)} %x.1), channel_id=1, source_target_pairs={{0,1},{1,0},{2,3},{3,2},{4,5},{5,4},{6,7},{7,6},{8,9},{9,8},{10,11... | collective-permute-start | bytes 1572872 | tf_op jit(solution)/shard_map/ppermute | solution.py:42
  10.8 16.6 %collective-permute-start = (bf16[1024,256]{1,0:T(8,128)(2,1)}, bf16[1024,256]{1,0:T(8,128)(2,1)S(1)}, u32[]{:S(2)}, u32[]{:S(2)}) collective-permute-start(bf16[1024,256]{1,0:T(8,128)(2,1)} %x.1), channel_id=1, source_target_pairs={{0,6},{2,0},{4,2},{6,4},{1,7},{3,1},{5,3},{7,5},{8,14},{10,8},{12,... | collective-permute-start | bytes 1572872 | tf_op jit(solution)/shard_map/ppermute | solution.py:38
  23.6 5.3 %collective-permute-start.4 = (bf16[1024,256]{1,0:T(8,128)(2,1)}, bf16[1024,256]{1,0:T(8,128)(2,1)S(1)}, u32[]{:S(2)}, u32[]{:S(2)}) collective-permute-start(bf16[1024,256]{1,0:T(8,128)(2,1)} %collective-permute-done.3.refs_2_), channel_id=1, source_target_pairs={{0,1},{1,0},{2,3},{3,2},{4,5},{5,4},{6,7},{7,6},{8,9},{9,8},{10,11... | collective-permute-start | bytes 1572872 | tf_op jit(solution)/shard_map/ppermute | solution.py:42
  23.7 8.1 %collective-permute-start.6 = (bf16[1024,256]{1,0:T(8,128)(2,1)S(1)}, bf16[1024,256]{1,0:T(8,128)(2,1)}, u32[]{:S(2)}, u32[]{:S(2)}) collective-permute-start(bf16[1024,256]{1,0:T(8,128)(2,1)S(1)} %collective-permute-done.5.refs_4_.x_p), channel_id=1, source_target_pairs={{0,1},{1,0},{2,3},{3,2},{4,5},{5,4},{6,7},{7,6},{8,9},{9,8},{10,11... | collective-permute-start | bytes 1572872 | tf_op jit(solution)/shard_map/ppermute | solution.py:42
  24.2 17.7 %collective-permute-start.7 = (bf16[1024,256]{1,0:T(8,128)(2,1)}, bf16[1024,256]{1,0:T(8,128)(2,1)S(1)}, u32[]{:S(2)}, u32[]{:S(2)}) collective-permute-start(bf16[1024,256]{1,0:T(8,128)(2,1)} %collective-permute-done.3.refs_2_), channel_id=1, source_target_pairs={{0,2},{2,4},{4,6},{6,0},{1,3},{3,5},{5,7},{7,1},{8,10},{10,12},{12... | collective-permute-start | bytes 1572872 | tf_op jit(solution)/shard_map/ppermute | solution.py:38
  24.8 17.1 %collective-permute-start.8 = (bf16[1024,256]{1,0:T(8,128)(2,1)S(1)}, bf16[1024,256]{1,0:T(8,128)(2,1)S(1)}, u32[]{:S(2)}, u32[]{:S(2)}) collective-permute-start(bf16[1024,256]{1,0:T(8,128)(2,1)S(1)} %collective-permute-done.5.refs_4_.x_p), channel_id=1, source_target_pairs={{0,6},{2,0},{4,2},{6,4},{1,7},{3,1},{5,3},{7,5},{8,14},{10,8},{12,... | collective-permute-start | bytes 1572872 | tf_op jit(solution)/shard_map/ppermute | solution.py:38
  27.4 14.5 %collective-permute-start.9 = (bf16[1024,256]{1,0:T(8,128)(2,1)}, bf16[1024,256]{1,0:T(8,128)(2,1)S(1)}, u32[]{:S(2)}, u32[]{:S(2)}) collective-permute-start(bf16[1024,256]{1,0:T(8,128)(2,1)} %collective-permute-done.3.refs_2_), channel_id=1, source_target_pairs={{0,8},{8,0},{1,9},{9,1},{2,10},{10,2},{3,11},{11,3},{4,12},{12,4},... | collective-permute-start | bytes 1572872 | tf_op jit(solution)/shard_map/ppermute | solution.py:42
  29.7 16.4 %collective-permute-start.1 = (bf16[1024,256]{1,0:T(8,128)(2,1)S(1)}, bf16[1024,256]{1,0:T(8,128)(2,1)S(1)}, u32[]{:S(2)}, u32[]{:S(2)}) collective-permute-start(bf16[1024,256]{1,0:T(8,128)(2,1)S(1)} %collective-permute-done.refs_0_), channel_id=1, source_target_pairs={{0,1},{1,0},{2,3},{3,2},{4,5},{5,4},{6,7},{7,6},{8,9},{9,8},{10,11... | collective-permute-start | bytes 1572872 | tf_op jit(solution)/shard_map/ppermute | solution.py:42
  43.0 6.3 %collective-permute-start.11 = (bf16[1024,256]{1,0:T(8,128)(2,1)}, bf16[1024,256]{1,0:T(8,128)(2,1)S(1)}, u32[]{:S(2)}, u32[]{:S(2)}) collective-permute-start(bf16[1024,256]{1,0:T(8,128)(2,1)} %get-tuple-element.42.refs_4_), channel_id=1, source_target_pairs={{0,1},{1,0},{2,3},{3,2},{4,5},{5,4},{6,7},{7,6},{8,9},{9,8},{10,11... | collective-permute-start | bytes 1572872 | tf_op jit(solution)/shard_map/ppermute | solution.py:42
  43.5 5.8 %collective-permute-start.12 = (bf16[1024,256]{1,0:T(8,128)(2,1)}, bf16[1024,256]{1,0:T(8,128)(2,1)S(1)}, u32[]{:S(2)}, u32[]{:S(2)}) collective-permute-start(bf16[1024,256]{1,0:T(8,128)(2,1)} %get-tuple-element.43.refs_6_), channel_id=1, source_target_pairs={{0,1},{1,0},{2,3},{3,2},{4,5},{5,4},{6,7},{7,6},{8,9},{9,8},{10,11... | collective-permute-start | bytes 1572872 | tf_op jit(solution)/shard_map/ppermute | solution.py:42
  43.6 5.8 %collective-permute-start.10 = (bf16[1024,256]{1,0:T(8,128)(2,1)}, bf16[1024,256]{1,0:T(8,128)(2,1)S(1)}, u32[]{:S(2)}, u32[]{:S(2)}) collective-permute-start(bf16[1024,256]{1,0:T(8,128)(2,1)} %get-tuple-element.41.refs_2_), channel_id=1, source_target_pairs={{0,1},{1,0},{2,3},{3,2},{4,5},{5,4},{6,7},{7,6},{8,9},{9,8},{10,11... | collective-permute-start | bytes 1572872 | tf_op jit(solution)/shard_map/ppermute | solution.py:42
  46.0 17.6 %collective-permute-start.13 = (bf16[512,256]{1,0:T(8,128)(2,1)S(1)}, bf16[512,256]{1,0:T(8,128)(2,1)S(1)}, u32[]{:S(2)}, u32[]{:S(2)}) collective-permute-start(bf16[512,256]{1,0:T(8,128)(2,1)S(1)} %slice.49), channel_id=1, source_target_pairs={{0,2},{2,4},{4,6},{6,0},{1,3},{3,5},{5,7},{7,1},{8,10},{10,12},{12... | collective-permute-start | bytes 786440 | tf_op jit(solution)/shard_map/ppermute | solution.py:38
  46.1 17.5 %collective-permute-start.14 = (bf16[512,256]{1,0:T(8,128)(2,1)S(1)}, bf16[512,256]{1,0:T(8,128)(2,1)S(1)}, u32[]{:S(2)}, u32[]{:S(2)}) collective-permute-start(bf16[512,256]{1,0:T(8,128)(2,1)S(1)} %slice.50), channel_id=1, source_target_pairs={{0,6},{2,0},{4,2},{6,4},{1,7},{3,1},{5,3},{7,5},{8,14},{10,8},{12,... | collective-permute-start | bytes 786440 | tf_op jit(solution)/shard_map/ppermute | solution.py:38
  64.4 2.1 collective-permute-start.16
  79.7 5.7 %collective-permute-start.17 = (f32[8,1024]{1,0:T(8,128)}, f32[8,1024]{1,0:T(8,128)S(1)}, u32[]{:S(2)}, u32[]{:S(2)}) collective-permute-start(f32[8,1024]{1,0:T(8,128)} %get-tuple-element.51), channel_id=1, source_target_pairs={{0,64},{64,0},{1,65},{65,1},{2,66},{66,2},{3,67},{67,3},{4,68},{68... | collective-permute-start | bytes 98312 | tf_op jit(solution)/shard_map/ppermute | solution.py:42
  86.1 4.7 %collective-permute-start.18 = (f32[2,8,1024]{2,1,0:T(8,128)S(1)}, f32[2,8,1024]{2,1,0:T(8,128)S(1)}, u32[]{:S(2)}, u32[]{:S(2)}) collective-permute-start(f32[2,8,1024]{2,1,0:T(8,128)S(1)} %pad_maximum_fusion.1.p0), channel_id=1, source_target_pairs={{0,16},{16,0},{32,48},{48,32},{1,17},{17,1},{33,49},{49,33},{2,18}... | collective-permute-start | bytes 196616 | tf_op jit(solution)/shard_map/ppermute | solution.py:42
  87.7 6.0 %collective-permute-start.19 = (f32[2,8,1024]{2,1,0:T(8,128)S(1)}, f32[2,8,1024]{2,1,0:T(8,128)S(1)}, u32[]{:S(2)}, u32[]{:S(2)}) collective-permute-start(f32[2,8,1024]{2,1,0:T(8,128)S(1)} %pad_maximum_fusion.1.p0), channel_id=1, source_target_pairs={{0,32},{16,48},{32,0},{48,16},{1,33},{17,49},{33,1},{49,17},{2,34}... | collective-permute-start | bytes 196616 | tf_op jit(solution)/shard_map/ppermute | solution.py:42
  90.6 5.5 %collective-permute-start.20 = (f32[2,8,1024]{2,1,0:T(8,128)S(1)}, f32[2,8,1024]{2,1,0:T(8,128)S(1)}, u32[]{:S(2)}, u32[]{:S(2)}) collective-permute-start(f32[2,8,1024]{2,1,0:T(8,128)S(1)} %pad_maximum_fusion.1.p0), channel_id=1, source_target_pairs={{0,48},{16,32},{32,16},{48,0},{1,49},{17,33},{33,17},{49,1},{2,50}... | collective-permute-start | bytes 196616 | tf_op jit(solution)/shard_map/ppermute | solution.py:42
  101.5 4.7 %collective-permute-start.22 = (f32[72,128]{1,0:T(8,128)S(1)}, f32[72,128]{1,0:T(8,128)S(1)}, u32[]{:S(2)}, u32[]{:S(2)}) collective-permute-start(f32[72,128]{1,0:T(8,128)S(1)} %add.79), channel_id=1, source_target_pairs={{0,2},{2,0},{4,6},{6,4},{1,3},{3,1},{5,7},{7,5},{8,10},{10,8},{12,... | collective-permute-start | bytes 110600 | tf_op jit(solution)/shard_map/ppermute | solution.py:42
  101.5 5.6 %collective-permute-start.23 = (f32[72,128]{1,0:T(8,128)S(1)}, f32[72,128]{1,0:T(8,128)S(1)}, u32[]{:S(2)}, u32[]{:S(2)}) collective-permute-start(f32[72,128]{1,0:T(8,128)S(1)} %add.79), channel_id=1, source_target_pairs={{0,4},{2,6},{4,0},{6,2},{1,5},{3,7},{5,1},{7,3},{8,12},{10,14},{12... | collective-permute-start | bytes 110600 | tf_op jit(solution)/shard_map/ppermute | solution.py:42
  103.1 5.2 %collective-permute-start.24 = (f32[72,128]{1,0:T(8,128)S(1)}, f32[72,128]{1,0:T(8,128)S(1)}, u32[]{:S(2)}, u32[]{:S(2)}) collective-permute-start(f32[72,128]{1,0:T(8,128)S(1)} %add.79), channel_id=1, source_target_pairs={{0,6},{2,4},{4,2},{6,0},{1,7},{3,5},{5,3},{7,1},{8,14},{10,12},{12... | collective-permute-start | bytes 110600 | tf_op jit(solution)/shard_map/ppermute | solution.py:42
  108.3 4.0 %collective-permute-start.25 = (f32[72,128]{1,0:T(8,128)S(1)}, f32[72,128]{1,0:T(8,128)S(1)}, u32[]{:S(2)}, u32[]{:S(2)}) collective-permute-start(f32[72,128]{1,0:T(8,128)S(1)} %add_add_fusion.part_a), channel_id=1, source_target_pairs={{0,8},{8,0},{1,9},{9,1},{2,10},{10,2},{3,11},{11,3},{4,12},{12,4},... | collective-permute-start | bytes 110600 | tf_op jit(solution)/shard_map/ppermute | solution.py:42
  128.6 10.3 %collective-permute-start.26 = (bf16[4,2,1024,256]{3,2,1,0:T(8,128)(2,1)}, bf16[4,2,1024,256]{3,2,1,0:T(8,128)(2,1)}, u32[]{:S(2)}, u32[]{:S(2)}) collective-permute-start(bf16[4,2,1024,256]{3,2,1,0:T(8,128)(2,1)} %term_part.2._), channel_id=1, source_target_pairs={{0,1},{1,0},{2,3},{3,2},{4,5},{5,4},{6,7},{7,6},{8,9},{9,8},{10,11... | collective-permute-start | bytes 12582920 | tf_op jit(solution)/shard_map/ppermute | solution.py:42
  150.0 18.3 %collective-permute-start.33 = (bf16[2,640,256]{2,1,0:T(8,128)(2,1)S(1)}, bf16[2,640,256]{2,1,0:T(8,128)(2,1)S(1)}, u32[]{:S(2)}, u32[]{:S(2)}) collective-permute-start(bf16[2,640,256]{2,1,0:T(8,128)(2,1)S(1)} %copy-done.15), channel_id=1, source_target_pairs={{0,16},{16,32},{32,48},{48,0},{1,17},{17,33},{33,49},{49,1},{2,18}... | collective-permute-start | bytes 1966088 | tf_op jit(solution)/shard_map/ppermute | solution.py:38
  150.0 19.7 %collective-permute-start.37 = (bf16[2,640,256]{2,1,0:T(8,128)(2,1)}, bf16[2,640,256]{2,1,0:T(8,128)(2,1)S(1)}, u32[]{:S(2)}, u32[]{:S(2)}) collective-permute-start(bf16[2,640,256]{2,1,0:T(8,128)(2,1)} %get-tuple-element.68), channel_id=1, source_target_pairs={{0,48},{16,0},{32,16},{48,32},{1,49},{17,1},{33,17},{49,33},{2,50}... | collective-permute-start | bytes 1966088 | tf_op jit(solution)/shard_map/ppermute | solution.py:38
  153.2 23.8 %collective-permute-start.35 = (bf16[2,2,360,256]{3,2,1,0:T(8,128)(2,1)}, bf16[2,2,360,256]{3,2,1,0:T(8,128)(2,1)S(1)}, u32[]{:S(2)}, u32[]{:S(2)}) collective-permute-start(bf16[2,2,360,256]{3,2,1,0:T(8,128)(2,1)} %get-tuple-element.64), channel_id=1, source_target_pairs={{0,64},{64,0},{1,65},{65,1},{2,66},{66,2},{3,67},{67,3},{4,68},{68... | collective-permute-start | bytes 2211848 | tf_op jit(solution)/shard_map/ppermute | solution.py:42
  169.6 17.7 %collective-permute-start.34 = (bf16[2,640,256]{2,1,0:T(8,128)(2,1)S(1)}, bf16[2,640,256]{2,1,0:T(8,128)(2,1)S(1)}, u32[]{:S(2)}, u32[]{:S(2)}) collective-permute-start(bf16[2,640,256]{2,1,0:T(8,128)(2,1)S(1)} %add.87), channel_id=1, source_target_pairs={{0,16},{16,32},{32,48},{48,0},{1,17},{17,33},{33,49},{49,1},{2,18}... | collective-permute-start | bytes 1966088 | tf_op jit(solution)/shard_map/ppermute | solution.py:38
  171.1 23.5 %collective-permute-start.38 = (bf16[2,640,256]{2,1,0:T(8,128)(2,1)S(1)}, bf16[2,640,256]{2,1,0:T(8,128)(2,1)S(1)}, u32[]{:S(2)}, u32[]{:S(2)}) collective-permute-start(bf16[2,640,256]{2,1,0:T(8,128)(2,1)S(1)} %add.89), channel_id=1, source_target_pairs={{0,48},{16,0},{32,16},{48,32},{1,49},{17,1},{33,17},{49,33},{2,50}... | collective-permute-start | bytes 1966088 | tf_op jit(solution)/shard_map/ppermute | solution.py:38
  174.3 24.8 %collective-permute-start.41 = (bf16[2,2,360,256]{3,2,1,0:T(8,128)(2,1)}, bf16[2,2,360,256]{3,2,1,0:T(8,128)(2,1)S(1)}, u32[]{:S(2)}, u32[]{:S(2)}) collective-permute-start(bf16[2,2,360,256]{3,2,1,0:T(8,128)(2,1)} %get-tuple-element.74), channel_id=1, source_target_pairs={{0,64},{64,0},{1,65},{65,1},{2,66},{66,2},{3,67},{67,3},{4,68},{68... | collective-permute-start | bytes 2211848 | tf_op jit(solution)/shard_map/ppermute | solution.py:42
  188.6 17.0 %collective-permute-start.36 = (bf16[2,640,256]{2,1,0:T(8,128)(2,1)S(1)}, bf16[2,640,256]{2,1,0:T(8,128)(2,1)S(1)}, u32[]{:S(2)}, u32[]{:S(2)}) collective-permute-start(bf16[2,640,256]{2,1,0:T(8,128)(2,1)S(1)} %add.88), channel_id=1, source_target_pairs={{0,16},{16,32},{32,48},{48,0},{1,17},{17,33},{33,49},{49,1},{2,18}... | collective-permute-start | bytes 1966088 | tf_op jit(solution)/shard_map/ppermute | solution.py:38
  189.9 34.6 %collective-permute-start.29 = (f32[8,128]{1,0:T(8,128)S(1)}, f32[8,128]{1,0:T(8,128)S(1)}, u32[]{:S(2)}, u32[]{:S(2)}) collective-permute-start(f32[8,128]{1,0:T(8,128)S(1)} %add.83), channel_id=1, source_target_pairs={{0,2},{2,0},{4,6},{6,4},{1,3},{3,1},{5,7},{7,5},{8,10},{10,8},{12,... | collective-permute-start | bytes 12296 | tf_op jit(solution)/shard_map/ppermute | solution.py:42
  190.6 33.9 %collective-permute-start.30 = (f32[8,128]{1,0:T(8,128)S(1)}, f32[8,128]{1,0:T(8,128)S(1)}, u32[]{:S(2)}, u32[]{:S(2)}) collective-permute-start(f32[8,128]{1,0:T(8,128)S(1)} %add.83), channel_id=1, source_target_pairs={{0,4},{2,6},{4,0},{6,2},{1,5},{3,7},{5,1},{7,3},{8,12},{10,14},{12... | collective-permute-start | bytes 12296 | tf_op jit(solution)/shard_map/ppermute | solution.py:42
  195.8 17.0 %collective-permute-start.39 = (bf16[2,640,256]{2,1,0:T(8,128)(2,1)S(1)}, bf16[2,640,256]{2,1,0:T(8,128)(2,1)S(1)}, u32[]{:S(2)}, u32[]{:S(2)}) collective-permute-start(bf16[2,640,256]{2,1,0:T(8,128)(2,1)S(1)} %add.90), channel_id=1, source_target_pairs={{0,48},{16,0},{32,16},{48,32},{1,49},{17,1},{33,17},{49,33},{2,50}... | collective-permute-start | bytes 1966088 | tf_op jit(solution)/shard_map/ppermute | solution.py:38
  199.1 28.3 %collective-permute-start.31 = (f32[8,128]{1,0:T(8,128)S(1)}, f32[8,128]{1,0:T(8,128)S(1)}, u32[]{:S(2)}, u32[]{:S(2)}) collective-permute-start(f32[8,128]{1,0:T(8,128)S(1)} %add.83), channel_id=1, source_target_pairs={{0,6},{2,4},{4,2},{6,0},{1,7},{3,5},{5,3},{7,1},{8,14},{10,12},{12... | collective-permute-start | bytes 12296 | tf_op jit(solution)/shard_map/ppermute | solution.py:42
  205.6 36.2 %collective-permute-start.42 = (bf16[2,360,256]{2,1,0:T(8,128)(2,1)S(1)}, bf16[2,360,256]{2,1,0:T(8,128)(2,1)S(1)}, u32[]{:S(2)}, u32[]{:S(2)}) collective-permute-start(bf16[2,360,256]{2,1,0:T(8,128)(2,1)S(1)} %get-tuple-element.77), channel_id=1, source_target_pairs={{0,16},{16,32},{32,48},{48,0},{1,17},{17,33},{33,49},{49,1},{2,18}... | collective-permute-start | bytes 1105928 | tf_op jit(solution)/shard_map/ppermute | solution.py:38
  216.6 3.6 %collective-permute-start.45 = (f32[1,256]{1,0:T(1,128)S(1)}, f32[1,256]{1,0:T(1,128)S(1)}, u32[]{:S(2)}, u32[]{:S(2)}) collective-permute-start(f32[1,256]{1,0:T(1,128)S(1)} %slice_bitcast_fusion.1), channel_id=1, source_target_pairs={{0,8},{8,0},{1,9},{9,1},{2,10},{10,2},{3,11},{11,3},{4,12},{12,4},... | collective-permute-start | bytes 3080 | tf_op jit(solution)/shard_map/ppermute | solution.py:42
  220.1 22.5 %collective-permute-start.44 = (bf16[2,360,256]{2,1,0:T(8,128)(2,1)S(1)}, bf16[2,360,256]{2,1,0:T(8,128)(2,1)S(1)}, u32[]{:S(2)}, u32[]{:S(2)}) collective-permute-start(bf16[2,360,256]{2,1,0:T(8,128)(2,1)S(1)} %get-tuple-element.76), channel_id=1, source_target_pairs={{0,48},{16,0},{32,16},{48,32},{1,49},{17,1},{33,17},{49,33},{2,50}... | collective-permute-start | bytes 1105928 | tf_op jit(solution)/shard_map/ppermute | solution.py:38
  224.5 20.9 %collective-permute-start.43 = (bf16[2,360,256]{2,1,0:T(8,128)(2,1)S(1)}, bf16[2,360,256]{2,1,0:T(8,128)(2,1)S(1)}, u32[]{:S(2)}, u32[]{:S(2)}) collective-permute-start(bf16[2,360,256]{2,1,0:T(8,128)(2,1)S(1)} %fusion.1), channel_id=1, source_target_pairs={{0,32},{16,48},{32,0},{48,16},{1,33},{17,49},{33,1},{49,17},{2,34}... | collective-permute-start | bytes 1105928 | tf_op jit(solution)/shard_map/ppermute | solution.py:38
  224.5 22.1 %collective-permute-start.40 = (bf16[2,640,256]{2,1,0:T(8,128)(2,1)S(1)}, bf16[2,640,256]{2,1,0:T(8,128)(2,1)S(1)}, u32[]{:S(2)}, u32[]{:S(2)}) collective-permute-start(bf16[2,640,256]{2,1,0:T(8,128)(2,1)S(1)} %pad_maximum_fusion), channel_id=1, source_target_pairs={{0,64},{64,0},{1,65},{65,1},{2,66},{66,2},{3,67},{67,3},{4,68},{68... | collective-permute-start | bytes 1966088 | tf_op jit(solution)/shard_map/ppermute | solution.py:42
  227.4 13.2 %collective-permute-start.46 = (f32[1,256]{1,0:T(1,128)S(1)}, f32[1,256]{1,0:T(1,128)S(1)}, u32[]{:S(2)}, u32[]{:S(2)}) collective-permute-start(f32[1,256]{1,0:T(1,128)S(1)} %fusion.3), channel_id=1, source_target_pairs={{0,64},{64,0},{1,65},{65,1},{2,66},{66,2},{3,67},{67,3},{4,68},{68... | collective-permute-start | bytes 3080 | tf_op jit(solution)/shard_map/ppermute | solution.py:42
  240.6 12.8 %collective-permute-start.27 = (bf16[1024,256]{1,0:T(8,128)(2,1)S(1)}, bf16[1024,256]{1,0:T(8,128)(2,1)S(1)}, u32[]{:S(2)}, u32[]{:S(2)}) collective-permute-start(bf16[1024,256]{1,0:T(8,128)(2,1)S(1)} %slice_bitcast_fusion), channel_id=1, source_target_pairs={{0,8},{8,0},{1,9},{9,1},{2,10},{10,2},{3,11},{11,3},{4,12},{12,4},... | collective-permute-start | bytes 1572872 | tf_op jit(solution)/shard_map/ppermute | solution.py:42
  241.8 11.0 %collective-permute-start.47 = (f32[1,256]{1,0:T(1,128)S(1)}, f32[1,256]{1,0:T(1,128)S(1)}, u32[]{:S(2)}, u32[]{:S(2)}) collective-permute-start(f32[1,256]{1,0:T(1,128)S(1)} %add.100), channel_id=1, source_target_pairs={{0,16},{16,0},{32,48},{48,32},{1,17},{17,1},{33,49},{49,33},{2,18}... | collective-permute-start | bytes 3080 | tf_op jit(solution)/shard_map/ppermute | solution.py:42
  242.6 10.2 %collective-permute-start.48 = (f32[1,256]{1,0:T(1,128)S(1)}, f32[1,256]{1,0:T(1,128)S(1)}, u32[]{:S(2)}, u32[]{:S(2)}) collective-permute-start(f32[1,256]{1,0:T(1,128)S(1)} %add.100), channel_id=1, source_target_pairs={{0,32},{16,48},{32,0},{48,16},{1,33},{17,49},{33,1},{49,17},{2,34}... | collective-permute-start | bytes 3080 | tf_op jit(solution)/shard_map/ppermute | solution.py:42
  245.4 7.4 %collective-permute-start.49 = (f32[1,256]{1,0:T(1,128)S(1)}, f32[1,256]{1,0:T(1,128)S(1)}, u32[]{:S(2)}, u32[]{:S(2)}) collective-permute-start(f32[1,256]{1,0:T(1,128)S(1)} %add.100), channel_id=1, source_target_pairs={{0,48},{16,32},{32,16},{48,0},{1,49},{17,33},{33,17},{49,1},{2,50}... | collective-permute-start | bytes 3080 | tf_op jit(solution)/shard_map/ppermute | solution.py:42
  246.6 6.8 %collective-permute-start.32 = (f32[8,128]{1,0:T(8,128)S(1)}, f32[8,128]{1,0:T(8,128)S(1)}, u32[]{:S(2)}, u32[]{:S(2)}) collective-permute-start(f32[8,128]{1,0:T(8,128)S(1)} %add_add_fusion.1.da), channel_id=1, source_target_pairs={{0,8},{8,0},{1,9},{9,1},{2,10},{10,2},{3,11},{11,3},{4,12},{12,4},... | collective-permute-start | bytes 12296 | tf_op jit(solution)/shard_map/ppermute | solution.py:42
  (45 other events, 379.0 us)
Sparse Core Ops, SparseCore 0:
  149.0 46.0 reduce-scatter.1
